TPU v7x, 32 devices: a whole 2x2x4 slice. The times are simulated.
32 devices in a mesh: ctx: 8 (over z, y), wa: 4 (over x, core).
Axes of the slice: x: 2, y: 2, z: 4, core: 2. Of those that a mesh axis runs over, the one named last changes fastest.
Arguments:
- layer_input: bfloat16 [4096, 1536], P('ctx'), may hold values from -6 to 6
- segment_ids: int32 [4096], P('ctx'), may hold values from 0 to 4, as said below
- expert_ids: int32 [4096, 2], P('ctx'), may hold values from 0 to 7, all different within a row; in each aligned block of 512 rows (0 to 511, 512 to 1023, ...) at most 256 rows name the same one
- norm_gain: float32 [1536], replicated, may hold values from 0.1 to 1.9
- query_weight: bfloat16 [1536, 1536], P(None, 'wa'), may hold values from -0.15625 to 0.15625
- key_weight: bfloat16 [1536, 512], P(None, 'wa'), may hold values from -0.15625 to 0.15625
- value_weight: bfloat16 [1536, 512], P(None, 'wa'), may hold values from -0.15625 to 0.15625
- output_weight: bfloat16 [1536, 1536], P('wa'), may hold values from -2.5 to 2.5
- ffn_gain: float32 [1536], replicated, may hold values from 0.1 to 1.9
- router_weight: bfloat16 [1536, 8], replicated, may hold values from -0.078125 to 0.078125
- gate_weight: bfloat16 [8, 1536, 1024], P(None, None, 'wa'), may hold values from -0.15625 to 0.15625
- up_weight: bfloat16 [8, 1536, 1024], P(None, None, 'wa'), may hold values from -0.15625 to 0.15625
- down_weight: bfloat16 [8, 1024, 1536], P(None, 'wa'), may hold values from -0.25 to 0.25
- cotangent: bfloat16 [4096, 1536], P('ctx'), may hold values from -6 to 6
Outputs:
- layer_output: float32 [4096, 1536], P('ctx')
- input_grad: float32 [4096, 1536], P('ctx')
- norm_gain_grad: float32 [1536], P('ctx')
- query_grad: float32 [1536, 1536], P('ctx', 'wa')
- key_grad: float32 [1536, 512], P('ctx', 'wa')
- value_grad: float32 [1536, 512], P('ctx', 'wa')
- output_grad: float32 [1536, 1536], P('wa', 'ctx')
- ffn_gain_grad: float32 [1536], P('ctx')
- router_grad: float32 [1536, 8], P('ctx')
- gate_grad: float32 [8, 1536, 1024], P(None, 'ctx', 'wa')
- up_grad: float32 [8, 1536, 1024], P(None, 'ctx', 'wa')
- down_grad: float32 [8, 1024, 1536], P(None, 'wa', 'ctx')
Inputs may be any that keep to these rules, and one draw needn't show every extreme that they name: `segment_ids`: segment ids never fall along the sequence; there are 5 documents, each of 64 tokens or more. `expert_ids`: among the 512 tokens of one index of ctx, no expert is named more than 256 times, a bound that some block reaches; a token's two experts differ.
All inputs are finite; a program needn't handle non-finite values.
Results may differ from a plain program's by a relative error of at most 0.03.
Values may be sent and summed in bfloat16 or wider, within the bound.
No kernel may reach another device: no remote copies, remote signals or barrier semaphores. Data moves between devices by JAX's collectives and lax.ppermute only.
A program may use at most 192 MiB of HBM per device.

v0:
```python
import functools

import jax
import jax.numpy as jnp
from jax import lax
from jax.experimental import pallas as pl
from jax.experimental.pallas import tpu as pltpu
from jax.sharding import PartitionSpec as P

H = 24
KV = 8
HD = 64
eps = 1e-05
NEG = -1e30
F32 = jnp.float32
BF = jnp.bfloat16
VLIM = 60 * 1024 * 1024
EXTRA = 16
NT = (((1,), (1,)), ((), ()))
TN = (((0,), (0,)), ((), ()))


def digits_of(n):
    out = []
    stride = 1
    while n > 1:
        if stride == 1 and n % 2 == 0:
            radix = 2
        elif n % 4 == 0:
            radix = 4
        else:
            radix = n
        out.append((stride, radix))
        stride *= radix
        n //= radix
    return out


def moved(n, digit, shift):
    stride, radix = digit
    pairs = []
    for i in range(n):
        d = (i // stride) % radix
        pairs.append((i, i + ((d + shift) % radix - d) * stride))
    return pairs


def hop(x, n, digit, shift=1):
    return lax.ppermute(x, "ctx", moved(n, digit, shift))


def other_core(x):
    return lax.ppermute(x, "wa", [(i, i ^ 1) for i in range(4)])


def other_chip(x):
    return lax.ppermute(x, "wa", [(i, i ^ 2) for i in range(4)])


def rel_keys(digits):
    keys = [()]
    for _, radix in digits:
        keys = [k + (r,) for r in range(radix) for k in keys]
    return keys


def set_digit(key, at, value):
    return key[:at] + (value,) + key[at + 1 :]


def gather_ctx(x, n, digits, order):
    blocks = {tuple(0 for _ in digits): x}
    for at in order:
        fresh = {}
        for key, block in blocks.items():
            moving = block
            for s in range(1, digits[at][1]):
                moving = hop(moving, n, digits[at])
                fresh[set_digit(key, at, s)] = moving
        blocks.update(fresh)
    return blocks


def scatter_sends(blocks, n, digit):
    return [blocks[0]] + [hop(blocks[r], n, digit, -r) for r in range(1, len(blocks))]


def total(parts):
    return functools.reduce(jnp.add, [x.astype(F32) for x in parts])


def cut(stack, radix):
    per = stack.shape[0] // radix
    return [stack[r * per : (r + 1) * per] for r in range(radix)]


def scatter_ctx(stack, n, order, hold=lambda at, xs: xs, kind=BF):
    moving = stack
    for at in reversed(range(len(order))):
        parts = scatter_sends(cut(moving, order[at][1]), n, order[at])
        parts = parts[:1] + list(hold(at, parts[1:]))
        moving = total(parts)
        if at:
            moving = moving.astype(kind)
    return moving[0]


def stack_kernel(places, *refs):
    for i, (at, unit) in enumerate(places):
        refs[-1][i] = refs[at][unit]


def stacked(pieces):
    arrays = []
    places = []
    for array, unit in pieces:
        at = next((i for i, x in enumerate(arrays) if x is array), None)
        if at is None:
            at = len(arrays)
            arrays.append(array)
        places.append((at, unit))
    shape = (len(pieces),) + arrays[0].shape[1:]
    return pl.pallas_call(
        functools.partial(stack_kernel, tuple(places)),
        out_shape=jax.ShapeDtypeStruct(shape, arrays[0].dtype),
        in_specs=vspec(len(arrays)),
        out_specs=vspec(1)[0],
        compiler_params=params(),
        name="stacked",
        cost_estimate=cost(1),
    )(*arrays)


def exchange_top(groups, n, digits):
    return [groups[0]] + [hop(groups[r], n, digits[-1], r) for r in range(1, len(groups))]


def exchange_rest(groups, n, digits):
    keys = rel_keys(digits[1:])
    n_up = len(keys)
    per = n_up // len(groups)
    parts = {i: (groups[i // per], i % per) for i in range(n_up)}
    for at in reversed(range(1, len(digits) - 1)):
        for s in range(1, digits[at][1]):
            chosen = [i for i, k in enumerate(keys) if k[at - 1] == s]
            bundle = hop(stacked([parts[i] for i in chosen]), n, digits[at], s)
            for place, i in enumerate(chosen):
                parts[i] = (bundle, place)
    return [parts[i] for i in range(n_up)]


def swapped(pieces, first):
    arrays = []
    for array, _ in pieces:
        if not any(array is x for x in arrays):
            arrays.append(array)
    held = tie(arrays, first)
    pieces = [(held[next(i for i, x in enumerate(arrays) if x is a)], u) for a, u in pieces]
    near = stacked(pieces)
    return near, other_core(near)


def digit_offset(me, key, digits, sign):
    place = 0
    for (stride, radix), r in zip(digits, key):
        d = (me // stride) % radix
        place = place + ((d + sign * r) % radix) * stride
    return place


def tie_kernel(*refs):
    pass


def tie(xs, first):
    xs, first = list(xs), list(first)
    return pl.pallas_call(
        tie_kernel,
        out_shape=tuple(jax.ShapeDtypeStruct(x.shape, x.dtype) for x in xs),
        in_specs=anywhere(len(xs) + len(first)),
        out_specs=tuple(anywhere(len(xs))),
        input_output_aliases={i: i for i in range(len(xs))},
        name="tie",
    )(*xs, *first)


def diagonal(x):
    return lax.ppermute(x, "wa", [(i, i ^ 3) for i in range(4)])


def all_parts(near, far):
    return [near, other_core(far), other_chip(near), diagonal(far)]


def cost(us):
    return pl.CostEstimate(flops=int(us * 3e8), bytes_accessed=int(us * 9e5), transcendentals=0)


def params(**kw):
    return pltpu.CompilerParams(vmem_limit_bytes=VLIM, **kw)


def vspec(n):
    return [pl.BlockSpec(memory_space=pltpu.VMEM)] * n


def drop_first(kernel, at, count):
    if not count:
        return kernel

    def waiting(*refs):
        kernel(*refs[:at], *refs[at + count :])

    return waiting


def anywhere(count):
    return [pl.BlockSpec(memory_space=pl.ANY)] * count


def project_kernel(core_ref, x_ref, gain_ref, wq_ref, wk_ref, wv_ref, extra_ref, a1_ref, q_ref, kv_ref):
    tok = x_ref.shape[0]
    half = tok // 2
    kvw = wk_ref.shape[1]
    for i in range(2):
        start = pl.multiple_of(((core_ref[0] + i) % 2) * half, half)
        x = x_ref[pl.ds(start, half), :].astype(F32)
        inv = lax.rsqrt(jnp.mean(x * x, axis=-1, keepdims=True) + eps)
        a1 = (x * inv * gain_ref[...][None, :]).astype(BF)
        rows = pl.ds(i * half, half)
        a1_ref[rows, :] = a1
        kv_ref[rows, :kvw] = jnp.dot(a1, wk_ref[...], preferred_element_type=F32).astype(BF)
        kv_ref[rows, kvw:] = jnp.dot(a1, wv_ref[...], preferred_element_type=F32).astype(BF)
        q = jnp.dot(a1, wq_ref[...], preferred_element_type=F32).astype(BF)
        q_ref[rows, :] = (q.astype(F32) * HD ** (-0.5)).astype(BF)
    kv_ref[pl.ds(tok, EXTRA), :] = extra_ref[...]


def project(core, x, gain, wq, wk, wv, extra):
    tok, width = x.shape
    return pl.pallas_call(
        project_kernel,
        out_shape=(
            jax.ShapeDtypeStruct((tok, width), BF),
            jax.ShapeDtypeStruct((tok, wq.shape[1]), BF),
            jax.ShapeDtypeStruct((tok + EXTRA, 2 * wk.shape[1]), BF),
        ),
        in_specs=[pl.BlockSpec(memory_space=pltpu.SMEM)] + vspec(6),
        out_specs=tuple(vspec(3)),
        compiler_params=params(),
        name="project",
        cost_estimate=cost(5),
    )(core, x, gain, wq, wk, wv, extra)


def seg_onehot(row):
    lane = lax.broadcasted_iota(jnp.int32, (16, row.shape[1]), 0).astype(F32)
    return jnp.where(lane == row, 1.0, 0.0).astype(BF)


def seg_rows_of(block, tok):
    width = block.shape[1]
    return [
        block[tok : tok + EXTRA, :].astype(F32)[i : i + 1, :] for i in range(tok // width)
    ]


ROWS = 256


def block_segs(block, tok):
    return jnp.concatenate(seg_rows_of(block, tok), axis=1)


def turned_groups(x, out, heads, groups):
    x = x.astype(F32).T.astype(BF)
    pairs = heads // groups
    for r in range(x.shape[1] // ROWS):
        for h in range(heads):
            n, g = h // groups, h % groups
            out[r * pairs + n, :, g * ROWS : (g + 1) * ROWS] = x[
                h * HD : (h + 1) * HD, r * ROWS : (r + 1) * ROWS
            ]


def straight_groups(x, out, heads, groups):
    pairs = heads // groups
    for r in range(x.shape[0] // ROWS):
        for h in range(heads):
            n, g = h // groups, h % groups
            out[r * pairs + n, g * ROWS : (g + 1) * ROWS, :] = x[
                r * ROWS : (r + 1) * ROWS, h * HD : (h + 1) * HD
            ]


def head_rows(ref, r, n, groups):
    rows = slice(r * ROWS, (r + 1) * ROWS)
    return jnp.concatenate(
        [ref[h : h + 1, rows] for h in range(n * groups, (n + 1) * groups)], axis=1
    )


def visit_tiles(kv_s, own, tok, body, before, behind):
    tiles = tok // ROWS
    lows = [jnp.min(own[:, r * ROWS : (r + 1) * ROWS]) for r in range(tiles)]
    highs = [jnp.max(own[:, r * ROWS : (r + 1) * ROWS]) for r in range(tiles)]

    def visit(b, carry):
        seg = block_segs(kv_s[b], tok)
        lo = jnp.min(seg)
        hi = jnp.max(seg)
        before(b)
        for r in range(tiles):
            plain = (lo == hi) & (lows[r] == highs[r]) & (lo == lows[r])
            touch = (lo <= highs[r]) & (lows[r] <= hi)
            pl.when(plain)(functools.partial(body, b, r, False))
            pl.when(touch & jnp.logical_not(plain))(functools.partial(body, b, r, True))
        behind(b)
        return carry

    lax.fori_loop(0, kv_s.shape[0], visit, 0)


def same_tile(block, own_hot, r, tok, groups):
    same = lax.dot_general(
        seg_onehot(block_segs(block, tok)),
        own_hot[:, r * ROWS : (r + 1) * ROWS],
        TN,
        preferred_element_type=F32,
    )
    return jnp.concatenate([same] * groups, axis=1) > 0.5


def attend_kernel(nb, heads, groups, *refs):
    q_ref = refs[0]
    kv_refs = refs[1 : 1 + nb]
    hf_ref, near_ref, far_ref, lse_ref = refs[1 + nb : 5 + nb]
    kv_s, q_s, m_s, acc_s = refs[5 + nb :]
    tok = q_ref.shape[0]
    kvw = kv_refs[0].shape[1] // 2
    pairs = heads // groups
    for b in range(nb):
        kv_s[b] = kv_refs[b][...]
    turned_groups(q_ref[...], q_s, heads, groups)
    own = block_segs(kv_s[0], tok)
    own_hot = seg_onehot(own)
    m_s[...] = jnp.full(m_s.shape, NEG, F32)
    acc_s[...] = jnp.zeros(acc_s.shape, F32)

    def body(b, r, masked):
        block = kv_s[b]
        if masked:
            same = same_tile(block, own_hot, r, tok, groups)
        scores = []
        for n in range(pairs):
            k = block[:tok, n * HD : (n + 1) * HD]
            s = jnp.dot(k, q_s[r * pairs + n], preferred_element_type=F32)
            scores.append(jnp.where(same, s, NEG) if masked else s)
        old = [m_s[r * pairs + n : r * pairs + n + 1, :] for n in range(pairs)]
        new = [
            jnp.maximum(old[n], jnp.max(scores[n], axis=0, keepdims=True)) for n in range(pairs)
        ]
        for n in range(pairs):
            i = r * pairs + n
            m_s[i : i + 1, :] = new[n]
            p = jnp.exp(scores[n] - new[n]).astype(BF)
            v = block[:tok, kvw + n * HD : kvw + (n + 1) * HD]
            v = jnp.concatenate([v, jnp.ones((tok, 16), BF)], axis=1)
            acc_s[i] = acc_s[i] * jnp.exp(old[n] - new[n]) + lax.dot_general(
                v, p, TN, preferred_element_type=F32
            )

    def nothing(b):
        pass

    visit_tiles(kv_s, own, tok, body, nothing, nothing)
    tiles = []
    for r in range(tok // ROWS):
        rows = []
        for n in range(pairs):
            i = r * pairs + n
            total = acc_s[i, HD : HD + 1, :]
            out = acc_s[i, :HD, :] / total
            lse = m_s[i : i + 1, :] + jnp.log(total)
            for g in range(groups):
                h = n * groups + g
                lanes = slice(g * ROWS, (g + 1) * ROWS)
                rows.append(out[:, lanes])
                lse_ref[h : h + 1, r * ROWS : (r + 1) * ROWS] = lse[:, lanes]
        tiles.append(jnp.concatenate(rows, axis=0))
    out = jnp.concatenate(tiles, axis=1).T
    hf_ref[...] = out
    near_ref[...] = out[: tok // 2].astype(BF)
    far_ref[...] = out[tok // 2 :].astype(BF)


def attend(q, blocks, heads, groups, first=()):
    tok = q.shape[0]
    nb = len(blocks)
    units = (tok // ROWS) * (heads // groups)
    return pl.pallas_call(
        drop_first(functools.partial(attend_kernel, nb, heads, groups), 1 + nb, len(first)),
        out_shape=(
            jax.ShapeDtypeStruct((tok, heads * HD), F32),
            jax.ShapeDtypeStruct((tok // 2, heads * HD), BF),
            jax.ShapeDtypeStruct((tok // 2, heads * HD), BF),
            jax.ShapeDtypeStruct((8, tok), F32),
        ),
        in_specs=vspec(1 + nb) + anywhere(len(first)),
        out_specs=tuple(vspec(4)),
        scratch_shapes=[
            pltpu.VMEM((nb,) + blocks[0].shape, BF),
            pltpu.VMEM((units, HD, groups * ROWS), BF),
            pltpu.VMEM((max(8, units), groups * ROWS), F32),
            pltpu.VMEM((units, HD + 16, groups * ROWS), F32),
        ],
        compiler_params=params(),
        name="attend",
        cost_estimate=cost(27),
    )(q, *blocks, *first)


def attend_back_kernel(nb, heads, groups, start, end, *refs):
    q_ref, own_ref, lse_ref = refs[:3]
    kv_refs = refs[3 : 3 + nb]
    at = 3 + nb
    if start:
        att_near_ref, att_far_ref, wo_ref, hf_ref = refs[at : at + 4]
        at += 4
    else:
        grad_in_ref, delta_in_ref, dq_in_ref = refs[at : at + 3]
        at += 3
    dkv_ref = refs[at]
    at += 1
    if start:
        grad_ref, delta_ref = refs[at : at + 2]
        at += 2
    if end:
        dq_near_ref, dq_far_ref = refs[at : at + 2]
        at += 2
    else:
        dq_out_ref = refs[at]
        at += 1
    kv_s, qt_s, q_s, dot_s, do_s, delta_s, dq_s, acc_s = refs[at:]
    tok = q_ref.shape[0]
    kvw = own_ref.shape[1] // 2
    key_heads = heads // groups
    if start:
        grad = jnp.concatenate(
            [
                lax.dot_general(ref[...], wo_ref[...], NT, preferred_element_type=F32)
                for ref in (att_near_ref, att_far_ref)
            ],
            axis=0,
        ).astype(BF)
        grad_ref[...] = grad
        prod = (grad.astype(F32) * hf_ref[...]).T
        for h in range(heads):
            delta_s[h : h + 1, :] = jnp.sum(prod[h * HD : (h + 1) * HD, :], axis=0, keepdims=True)
        delta_ref[...] = delta_s[...]
        dq_s[...] = jnp.zeros(dq_s.shape, F32)
    else:
        grad = grad_in_ref[...]
        delta_s[...] = delta_in_ref[...]
        dq_s[...] = dq_in_ref[...]
    for b in range(nb):
        kv_s[b] = kv_refs[b][...]
    turned_groups(q_ref[...], qt_s, heads, groups)
    straight_groups(q_ref[...], q_s, heads, groups)
    turned_groups(grad, dot_s, heads, groups)
    straight_groups(grad, do_s, heads, groups)
    own = block_segs(own_ref[...], tok)
    own_hot = seg_onehot(own)

    def body(b, r, masked):
        block = kv_s[b]
        if masked:
            same = same_tile(block, own_hot, r, tok, groups)
        for n in range(key_heads):
            i = r * key_heads + n
            k = block[:tok, n * HD : (n + 1) * HD]
            v = block[:tok, kvw + n * HD : kvw + (n + 1) * HD]
            s = jnp.dot(k, qt_s[i], preferred_element_type=F32)
            dp = jnp.dot(v, dot_s[i], preferred_element_type=F32)
            p = jnp.exp(s - head_rows(lse_ref, r, n, groups))
            if masked:
                p = jnp.where(same, p, 0.0)
            ds = (p * (dp - head_rows(delta_s, r, n, groups))).astype(BF)
            acc_s[n] += jnp.dot(ds, q_s[i], preferred_element_type=F32)
            acc_s[key_heads + n] += jnp.dot(p.astype(BF), do_s[i], preferred_element_type=F32)
            dq_s[i] += lax.dot_general(k, ds, TN, preferred_element_type=F32)

    def before(b):
        acc_s[...] = jnp.zeros(acc_s.shape, F32)

    def behind(b):
        sums = jnp.concatenate([acc_s[i] for i in range(2 * key_heads)], axis=1)
        dkv_ref[b] = sums.astype(BF)

    visit_tiles(kv_s, own, tok, body, before, behind)
    if end:
        tiles = []
        for r in range(tok // ROWS):
            rows = [
                dq_s[r * key_heads + h // groups, :, (h % groups) * ROWS : (h % groups + 1) * ROWS]
                for h in range(heads)
            ]
            tiles.append(jnp.concatenate(rows, axis=0))
        out = (jnp.concatenate(tiles, axis=1).T * HD ** (-0.5)).astype(BF)
        dq_near_ref[...] = out[: tok // 2]
        dq_far_ref[...] = out[tok // 2 :]
    else:
        dq_out_ref[...] = dq_s[...]


def attend_back(q, own, lse, blocks, heads, groups, start=None, going=None, end=True, first=()):
    tok = q.shape[0]
    nb = len(blocks)
    width = heads * HD
    key_heads = heads // groups
    units = (tok // ROWS) * key_heads
    operands = [q, own, lse] + list(blocks) + list(start if start is not None else going)
    outs = [((nb, tok, own.shape[1]), BF)]
    if start is not None:
        outs += [((tok, width), BF), ((8, tok), F32)]
    outs += [((tok // 2, width), BF)] * 2 if end else [((units, HD, groups * ROWS), F32)]
    kernel = functools.partial(
        attend_back_kernel, nb, heads, groups, start is not None, end
    )
    return pl.pallas_call(
        drop_first(kernel, len(operands), len(first)),
        out_shape=tuple(jax.ShapeDtypeStruct(shape, dtype) for shape, dtype in outs),
        in_specs=vspec(len(operands)) + anywhere(len(first)),
        out_specs=tuple(vspec(len(outs))),
        scratch_shapes=[
            pltpu.VMEM((nb,) + blocks[0].shape, BF),
            pltpu.VMEM((units, HD, groups * ROWS), BF),
            pltpu.VMEM((units, groups * ROWS, HD), BF),
            pltpu.VMEM((units, HD, groups * ROWS), BF),
            pltpu.VMEM((units, groups * ROWS, HD), BF),
            pltpu.VMEM((8, tok), F32),
            pltpu.VMEM((units, HD, groups * ROWS), F32),
            pltpu.VMEM((2 * key_heads, tok, HD), F32),
        ],
        compiler_params=params(),
        name="attend_back",
        cost_estimate=cost(4.5 * nb),
    )(*operands, *first)


def routes_kernel(at, *refs):
    out_ref = refs[-1]
    tok = out_ref.shape[1]
    for b, ref in enumerate(refs[:-1]):
        rows = ref[tok : tok + EXTRA, :].astype(F32)
        both = [
            jnp.concatenate([rows[i : i + 1, :] for i in range(c * at, (c + 1) * at)], axis=1)
            for c in (1, 2)
        ]
        out_ref[b] = jnp.concatenate(both + [jnp.zeros((6, tok), F32)], axis=0).T


def routes(blocks, tok, first=()):
    return pl.pallas_call(
        drop_first(
            functools.partial(routes_kernel, tok // blocks[0].shape[1]), len(blocks), len(first)
        ),
        out_shape=jax.ShapeDtypeStruct((len(blocks), tok, 8), F32),
        in_specs=vspec(len(blocks)) + anywhere(len(first)),
        out_specs=vspec(1)[0],
        compiler_params=params(),
        name="routes",
        cost_estimate=cost(2),
    )(*blocks, *first)


def experts_kernel(
    core_ref,
    ids_ref,
    mine_ref,
    theirs_ref,
    g_ref,
    wr_ref,
    wg_ref,
    wu_ref,
    wd_ref,
    mix_keep_ref,
    mix_send_ref,
    dx_keep_ref,
    dx_send_ref,
    gates_ref,
    ent_ref,
    a2_s,
    g_s,
    mix_s,
    dx_s,
    back_s,
):
    e = pl.program_id(0)
    tok, width = a2_s.shape
    half = tok // 2
    experts = wr_ref.shape[0]
    lane = lax.broadcasted_iota(jnp.int32, (tok, experts), 1)
    first = ids_ref[:, 0:1]
    second = ids_ref[:, 1:2]

    @pl.when(e == 0)
    def _():
        a2_s[:half, :] = mine_ref[...]
        a2_s[half:, :] = theirs_ref[...]
        for i in range(2):
            start = pl.multiple_of(((core_ref[0] + i) % 2) * half, half)
            g_s[pl.ds(i * half, half), :] = g_ref[pl.ds(start, half), :]
        logits = lax.dot_general(a2_s[...], wr_ref[...], NT, preferred_element_type=F32)
        one = jnp.sum(jnp.where(lane == first, logits, 0.0), axis=1, keepdims=True)
        two = jnp.sum(jnp.where(lane == second, logits, 0.0), axis=1, keepdims=True)
        top = jnp.maximum(one, two)
        one = jnp.exp(one - top)
        two = jnp.exp(two - top)
        total = one + two
        gates_ref[...] = jnp.where(lane == first, one / total, 0.0) + jnp.where(
            lane == second, two / total, 0.0
        )
        mix_s[...] = jnp.zeros(mix_s.shape, F32)
        dx_s[...] = jnp.zeros(dx_s.shape, F32)
        back_s[...] = jnp.zeros(back_s.shape, F32)
        ent_ref[...] = jnp.zeros(ent_ref.shape, BF)

    wg = wg_ref[0]
    wu = wu_ref[0]
    wd = wd_ref[0]
    for i in range(2):
        rows = pl.ds(i * half, half)
        a2 = a2_s[rows, :]
        u = jnp.dot(a2, wg, preferred_element_type=F32)
        w = jnp.dot(a2, wu, preferred_element_type=F32)
        m = lax.dot_general(g_s[rows, :], wd, NT, preferred_element_type=F32)
        here = lane[:half] == e
        gate = jnp.sum(jnp.where(here, gates_ref[rows, :], 0.0), axis=1, keepdims=True)
        pick_one = (ids_ref[rows, 0:1] == e).astype(F32)
        pick_two = (ids_ref[rows, 1:2] == e).astype(F32)
        sig = 1.0 / (1.0 + jnp.exp(-u))
        act = u * sig
        mid = (act * w).astype(BF).astype(F32)
        back = jnp.sum(mid * m, axis=1, keepdims=True) * (pick_one + pick_two)
        back_s[rows, :] += jnp.where(here, back, 0.0)
        mid = mid * gate
        gm = gate * m
        up_back = gm * act
        pre_back = gm * w * sig * (1.0 + u * (1.0 - sig))
        mid_b = mid.astype(BF)
        up_b = up_back.astype(BF)
        pre_b = pre_back.astype(BF)
        mix_s[rows, :] += jnp.dot(mid_b, wd, preferred_element_type=F32)
        dx_s[rows, :] += lax.dot_general(
            pre_b, wg, NT, preferred_element_type=F32
        ) + lax.dot_general(up_b, wu, NT, preferred_element_type=F32)
        for kind, value in enumerate((mid, pre_back, up_back)):
            for c, pick in enumerate((pick_one, pick_two)):
                ent_ref[2 * kind + c, rows, :] += (value * pick).astype(BF)

    @pl.when(e == pl.num_programs(0) - 1)
    def _():
        mix_keep_ref[...] = mix_s[:half, :]
        mix_send_ref[...] = mix_s[half:, :].astype(BF)
        dx_keep_ref[:, :width] = dx_s[:half, :]
        dx_send_ref[:, :width] = dx_s[half:, :].astype(BF)
        pad = jnp.zeros((half, 128 - experts), F32)
        dx_keep_ref[:, width:] = jnp.concatenate([back_s[:half, :], pad], axis=1)
        dx_send_ref[:, width:] = jnp.concatenate([back_s[half:, :], pad], axis=1).astype(BF)


def experts_call(core, ids, mine, theirs, g, wr, wg, wu, wd, first=()):
    half, width = mine.shape
    tok = 2 * half
    experts, _, hidden = wg.shape

    def whole(*shape):
        return pl.BlockSpec(shape, lambda e, *_: (0,) * len(shape))

    def one(*shape):
        return pl.BlockSpec((1,) + shape, lambda e, *_: (e,) + (0,) * len(shape))

    return pl.pallas_call(
        drop_first(experts_kernel, 9, len(first)),
        out_shape=(
            jax.ShapeDtypeStruct((half, width), F32),
            jax.ShapeDtypeStruct((half, width), BF),
            jax.ShapeDtypeStruct((half, width + 128), F32),
            jax.ShapeDtypeStruct((half, width + 128), BF),
            jax.ShapeDtypeStruct((tok, experts), F32),
            jax.ShapeDtypeStruct((6, tok, hidden), BF),
        ),
        grid=(experts,),
        in_specs=[
            pl.BlockSpec(memory_space=pltpu.SMEM),
            whole(tok, 2),
            whole(half, width),
            whole(half, width),
            whole(tok, width),
            whole(experts, width),
            one(width, hidden),
            one(width, hidden),
            one(hidden, width),
        ]
        + anywhere(len(first)),
        out_specs=(
            whole(half, width),
            whole(half, width),
            whole(half, width + 128),
            whole(half, width + 128),
            whole(tok, experts),
            whole(6, tok, hidden),
        ),
        scratch_shapes=[
            pltpu.VMEM((tok, width), BF),
            pltpu.VMEM((tok, width), BF),
            pltpu.VMEM((tok, width), F32),
            pltpu.VMEM((tok, width), F32),
            pltpu.VMEM((tok, experts), F32),
        ],
        compiler_params=params(dimension_semantics=("arbitrary",)),
        name="experts",
        cost_estimate=cost(32),
    )(core, ids, mine, theirs, g, wr, wg, wu, wd, *first)


def expert_grads_kernel(count, base, places, ids_ref, *refs):
    x_refs = refs[0:2]
    g_refs = refs[2:4]
    ents = refs[4 : 4 + count]
    outs, theirs_ref = refs[-4:-1], refs[-1]
    e = (pl.program_id(0) + base).astype(F32)
    cols = outs[0].shape[1]
    sums = [None, None, None]
    for b in range(count):
        half = x_refs[0].shape[2]
        hidden = ents[b].shape[2]
        for i in range(2):
            rows = pl.ds(i * half, half)
            one = jnp.where(ids_ref[places[b], rows, 0:1] == e, 1.0, 0.0).astype(BF)
            two = jnp.where(ids_ref[places[b], rows, 1:2] == e, 1.0, 0.0).astype(BF)
            one = jnp.broadcast_to(one, (half, hidden))
            two = jnp.broadcast_to(two, (half, hidden))
            xt = x_refs[i][b]
            gt = g_refs[i][b]
            for kind in range(3):
                value = ents[b][2 * kind, rows, :] * one + ents[b][2 * kind + 1, rows, :] * two
                term = jnp.dot(gt if kind == 0 else xt, value, preferred_element_type=F32)
                sums[kind] = term if sums[kind] is None else sums[kind] + term
    for kind in range(3):
        outs[kind][0] = sums[kind][:cols]
        theirs_ref[kind, 0] = sums[kind][cols:].astype(BF)


def expert_grads(base, experts, ids, places, xm, xo, gm, go, ents, first=()):
    cols = xm.shape[1] // 2
    hidden = ents[0].shape[-1]
    operands = [ids, xm, xo, gm, go] + list(ents)
    specs = [pl.BlockSpec(x.shape, lambda e, nd=x.ndim: (0,) * nd) for x in operands]
    out_spec = pl.BlockSpec((1, cols, hidden), lambda e: (e, 0, 0))
    kernel = functools.partial(expert_grads_kernel, len(ents), base, places)
    return pl.pallas_call(
        drop_first(kernel, len(operands), len(first)),
        out_shape=(jax.ShapeDtypeStruct((experts, cols, hidden), F32),) * 3
        + (jax.ShapeDtypeStruct((3, experts, cols, hidden), BF),),
        grid=(experts,),
        in_specs=specs + anywhere(len(first)),
        out_specs=(out_spec,) * 3
        + (pl.BlockSpec((3, 1, cols, hidden), lambda e: (0, e, 0, 0)),),
        compiler_params=params(dimension_semantics=("arbitrary",)),
        name="expert_grads",
        cost_estimate=cost(1.2 * experts),
    )(*operands, *first)


def finish_kernel(*refs):
    mine, got_ref, outs = refs[:3], refs[3], refs[-3:]
    for kind in range(3):
        value = mine[kind][0] + got_ref[kind, 0].astype(F32)
        outs[kind][0] = value


def finish(base, experts, mine, got, outs=None, first=()):
    some, cols, hidden = mine[0].shape
    kept = [] if outs is None else list(outs)
    part = pl.BlockSpec((1, cols, hidden), lambda e: (e, 0, 0))
    place = pl.BlockSpec((1, cols, hidden), lambda e: (base + e, 0, 0))
    waits = kept + list(first)
    return pl.pallas_call(
        drop_first(finish_kernel, 4, len(waits)),
        out_shape=(jax.ShapeDtypeStruct((experts, cols, hidden), F32),) * 3,
        grid=(some,),
        in_specs=[part] * 3
        + [pl.BlockSpec((3, 1, cols, hidden), lambda e: (0, e, 0, 0))]
        + anywhere(len(waits)),
        out_specs=(place,) * 3,
        input_output_aliases={4 + i: i for i in range(len(kept))},
        compiler_params=params(dimension_semantics=("arbitrary",)),
        name="finish",
        cost_estimate=cost(3),
    )(*mine, got, *waits)


def my_rows(core_ref, ref):
    half = ref.shape[0] // 2
    return ref[pl.ds(pl.multiple_of(core_ref[0] * half, half), half), :]


def simple(kernel, name, outs, core, *operands, first=()):
    return pl.pallas_call(
        drop_first(kernel, 1 + len(operands), len(first)),
        out_shape=tuple(jax.ShapeDtypeStruct(shape, dtype) for shape, dtype in outs),
        in_specs=[pl.BlockSpec(memory_space=pltpu.SMEM)] + vspec(len(operands)) + anywhere(len(first)),
        out_specs=tuple(vspec(len(outs))),
        compiler_params=params(),
        name=name,
        cost_estimate=cost(5),
    )(core, *operands, *first)


def middle_kernel(core_ref, x_ref, gain_ref, *refs):
    parts, weights = refs[:4], refs[4:8]
    hidden_ref, a2_ref = refs[8:]
    total = my_rows(core_ref, x_ref).astype(F32)
    for part, weight in zip(parts, weights):
        total = total + jnp.dot(part[...], weight[...], preferred_element_type=F32)
    inv = lax.rsqrt(jnp.mean(total * total, axis=-1, keepdims=True) + eps)
    hidden_ref[...] = total
    a2_ref[...] = (total * inv * gain_ref[...][None, :]).astype(BF)


def back_kernel(
    core_ref,
    near_ref,
    got_ref,
    hidden_ref,
    a2_ref,
    gates_ref,
    ids_ref,
    wr_ref,
    gain_ref,
    g_ref,
    grad_ref,
    att_ref,
    misc_ref,
):
    half, width = hidden_ref.shape
    experts = wr_ref.shape[0]
    total = near_ref[...].astype(F32) + got_ref[...].astype(F32)
    gate_back = total[:, width:][:, :experts]
    gates = gates_ref[:half, :]
    lane = lax.broadcasted_iota(jnp.int32, (half, experts), 1)
    picked = (lane == ids_ref[:half, 0:1]) | (lane == ids_ref[:half, 1:2])
    logit = gates * (gate_back - jnp.sum(gates * gate_back, axis=-1, keepdims=True))
    logit = jnp.where(picked, logit, 0.0).astype(BF)
    back = total[:, :width] + jnp.dot(logit, wr_ref[...], preferred_element_type=F32)
    hidden = hidden_ref[...]
    inv = lax.rsqrt(jnp.mean(hidden * hidden, axis=-1, keepdims=True) + eps)
    upstream = my_rows(core_ref, g_ref).astype(F32)
    scaled = back * gain_ref[...][None, :]
    grad = upstream + inv * (
        scaled - hidden * inv * inv * jnp.mean(scaled * hidden, axis=-1, keepdims=True)
    )
    grad_ref[...] = grad
    att_ref[...] = grad.astype(BF)
    misc_ref[:8, :] = lax.dot_general(logit, a2_ref[...], TN, preferred_element_type=F32)
    ffn = jnp.sum(back * hidden * inv, axis=0, keepdims=True)
    misc_ref[8:, :] = jnp.broadcast_to(ffn, (8, width))


def query_back_kernel(core_ref, *refs):
    pairs, weights, out_ref = refs[:2], refs[2:6], refs[6]
    total = None
    for i, weight in enumerate(weights):
        term = lax.dot_general(
            pairs[i // 2][i % 2], weight[...], NT, preferred_element_type=F32
        )
        total = term if total is None else total + term
    out_ref[...] = total


def input_kernel(core_ref, x_ref, gain_ref, grad_ref, query_ref, *refs):
    parts, weights = refs[:4], refs[4:8]
    out_ref, norm_ref = refs[8:]
    back = query_ref[...]
    for part, weight in zip(parts, weights):
        start = weight.shape[1] - part.shape[1]
        back = back + lax.dot_general(
            part[...], weight[:, start:], NT, preferred_element_type=F32
        )
    x = my_rows(core_ref, x_ref).astype(F32)
    inv = lax.rsqrt(jnp.mean(x * x, axis=-1, keepdims=True) + eps)
    scaled = back * gain_ref[...][None, :]
    out_ref[...] = grad_ref[...] + inv * (
        scaled - x * inv * inv * jnp.mean(scaled * x, axis=-1, keepdims=True)
    )
    norm = jnp.sum(back * x * inv, axis=0, keepdims=True)
    norm_ref[...] = jnp.broadcast_to(norm, norm_ref.shape)


def place_kernel(core_ref, mine_ref, theirs_ref, out_ref):
    half = mine_ref.shape[0]
    out_ref[pl.ds(pl.multiple_of(core_ref[0] * half, half), half), :] = mine_ref[...]
    out_ref[pl.ds(pl.multiple_of((1 - core_ref[0]) * half, half), half), :] = theirs_ref[...]


def columns_kernel(waits, owner_ref, core_ref, x_ref, *refs):
    outs, turned = refs[waits:-1], refs[-1]
    per, rows_out, half = outs[0].shape
    side = owner_ref.shape[0] // (per * len(outs))
    cols = rows_out // side
    x = my_rows(core_ref, x_ref) if x_ref.shape[0] != half else x_ref[...]
    turned[...] = x.T
    for r, out_ref in enumerate(outs):
        for i in range(per * side):
            rows = pl.ds(pl.multiple_of(owner_ref[r * per * side + i] * cols, 16), cols)
            out_ref[i // side, (i % side) * cols : (i % side + 1) * cols, :] = turned[rows, :]


def columns(owner, core, x, half, groups, side, first=()):
    n = owner.shape[0]
    width = x.shape[1]
    smem = pl.BlockSpec(memory_space=pltpu.SMEM)
    out = jax.ShapeDtypeStruct((n // (groups * side), side * (width // n), half), BF)
    return pl.pallas_call(
        functools.partial(columns_kernel, len(first)),
        out_shape=(out,) * groups,
        in_specs=[smem, smem] + vspec(1) + [pl.BlockSpec(memory_space=pl.ANY)] * len(first),
        out_specs=tuple(vspec(groups)),
        scratch_shapes=[pltpu.VMEM((width, half), BF)],
        compiler_params=params(),
        name="columns",
        cost_estimate=cost(2.5),
    )(owner, core, x, *first)


def weight_kernel(shape, extra, owner_ref, *refs):
    out_ref, turned, misc_turned = refs[-3:]
    n, cols, _ = out_ref.shape
    at = 0
    column = 0
    for group, pairs in enumerate(shape):
        lefts, rights = refs[at : at + pairs], refs[at + pairs : at + 2 * pairs]
        at += 2 * pairs
        row = 0
        for left in lefts:
            turned[group, :, row : row + left.shape[0]] = left[...].T
            row += left.shape[0]
        right = jnp.concatenate([r[...] for r in rights], axis=0) if pairs > 1 else rights[0][...]
        for i in range(n):
            rows = pl.ds(pl.multiple_of(owner_ref[i] * cols, 16), cols)
            out_ref[i, :, column : column + right.shape[1]] = jnp.dot(
                turned[group, rows, :], right, preferred_element_type=F32
            ).astype(BF)
        column += right.shape[1]
    if extra:
        misc = refs[at][...]
        spare = jnp.zeros((128 - misc.shape[0], misc.shape[1]), F32)
        misc_turned[...] = jnp.concatenate([misc, spare], axis=0).T
        for i in range(n):
            rows = pl.ds(pl.multiple_of(owner_ref[i] * cols, 16), cols)
            out_ref[i, :, column:] = misc_turned[rows, :].astype(BF)


def weight_terms(owner, groups, misc=None, us=4, first=()):
    n = owner.shape[0]
    width = groups[0][0][0].shape[1]
    rows = sum(x.shape[0] for x in groups[0][0])
    out_width = sum(rights[0].shape[1] for _, rights in groups)
    operands = []
    for lefts, rights in groups:
        operands += list(lefts) + list(rights)
    if misc is not None:
        operands.append(misc)
        out_width += 128
    shape = tuple(len(lefts) for lefts, _ in groups)
    return pl.pallas_call(
        drop_first(
            functools.partial(weight_kernel, shape, misc is not None),
            1 + len(operands),
            len(first),
        ),
        out_shape=jax.ShapeDtypeStruct((n, width // n, out_width), BF),
        in_specs=[pl.BlockSpec(memory_space=pltpu.SMEM)]
        + vspec(len(operands))
        + anywhere(len(first)),
        out_specs=vspec(1)[0],
        scratch_shapes=[pltpu.VMEM((len(groups), width, rows), BF), pltpu.VMEM((width, 128), F32)],
        compiler_params=params(),
        name="weight_terms",
        cost_estimate=cost(us),
    )(owner, *operands, *first)


def per_device(
    n_ctx,
    layer_input,
    segment_ids,
    expert_ids,
    norm_gain,
    query_weight,
    key_weight,
    value_weight,
    output_weight,
    ffn_gain,
    router_weight,
    gate_weight,
    up_weight,
    down_weight,
    cotangent,
):
    tok, width = layer_input.shape
    half = tok // 2
    groups = H // KV
    kv_local = key_weight.shape[1] // HD
    heads = kv_local * groups
    kvw = key_weight.shape[1]
    experts = gate_weight.shape[0]
    cols = width // n_ctx
    digits = digits_of(n_ctx)
    keys = rel_keys(digits)
    upper_first = list(range(1, len(digits))) + [0]
    lower_first = list(range(len(digits)))
    me = lax.axis_index("ctx")
    core = lax.axis_index("wa") % 2
    core_arr = jnp.full((1,), core, jnp.int32)
    owner_to = jnp.stack([digit_offset(me, k, digits, 1) for k in keys]).astype(jnp.int32)
    owner_from = jnp.stack([digit_offset(me, k, digits, -1) for k in keys]).astype(jnp.int32)
    gain_one, gain_two = norm_gain, ffn_gain
    router = router_weight.T

    def mine_first(x):
        return jnp.where(core == 0, x, jnp.concatenate([x[half:], x[:half]], axis=0))

    segs = mine_first(segment_ids).astype(BF)
    ids = mine_first(expert_ids)
    extra = jnp.concatenate([segs, ids[:, 0].astype(BF), ids[:, 1].astype(BF)])
    extra = jnp.pad(extra, (0, EXTRA * 2 * kvw - extra.shape[0])).reshape(EXTRA, 2 * kvw)
    a1, q, kv = project(
        core_arr, layer_input, gain_one, query_weight, key_weight, value_weight, extra
    )
    tops = digits[-1][1]
    staged = len(digits) == 2
    side = digits[0][1]
    low, top = digits[0], digits[-1]
    turned_digits = digits[1:] + digits[:1]
    turned_keys = [(k[-1],) + k[:-1] for k in rel_keys(turned_digits)]
    owner_turned = jnp.stack(
        [digit_offset(me, k, digits, -1) for k in turned_keys]
    ).astype(jnp.int32)

    wo_chip = other_chip(output_weight)
    kv_weight = jnp.concatenate([key_weight, value_weight], axis=1)
    kv_core = other_core(kv_weight)
    g_out = columns(owner_to, core_arr, cotangent, half, tops, side, [kv])
    if staged:
        z, y = [kv], []
        for r in range(tops - 1):
            aside = [g_out[0], kv_core] if r == tops - 2 else []
            z_next, y_next = tie([hop(z[r], n_ctx, top), hop(z[r], n_ctx, low)], aside)
            z.append(z_next)
            y.append(y_next)
        y.append(hop(z[-1], n_ctx, low))
        kv_list = [block for pair in zip(z, y) for block in pair]
    else:
        kv_blocks = gather_ctx(kv, n_ctx, digits, upper_first)
        kv_list = [kv_blocks[k] for k in keys]

    g_top = exchange_top(g_out, n_ctx, digits)

    heads_f32, heads_near, heads_far, lse = attend(
        q, kv_list, heads, groups, first=[g_out[0]]
    )
    heads_near, heads_far, wo_chip, *rest = tie(
        [heads_near, heads_far, wo_chip] + list(g_top[1:]), []
    )
    g_top = [g_top[0]] + list(rest)
    wo_parts = [output_weight, other_core(output_weight), wo_chip, other_core(wo_chip)]

    parts = all_parts(heads_near, heads_far)
    g_pieces = exchange_rest(g_top, n_ctx, digits)
    hidden_one, a2_mine = simple(
        middle_kernel,
        "middle",
        [((half, width), F32), ((half, width), BF)],
        core_arr,
        layer_input,
        gain_two,
        *parts,
        *wo_parts,
    )
    a2_far = other_core(a2_mine)
    a2_out = columns(owner_to, core_arr, a2_mine, half, tops, side)
    a2_top = exchange_top(a2_out, n_ctx, digits)
    wq_chip = other_chip(query_weight)

    mix_keep, mix_send, dx_keep, dx_send, gates, ent = experts_call(
        core_arr,
        ids,
        a2_mine,
        a2_far,
        cotangent,
        router,
        gate_weight,
        up_weight,
        down_weight,
        first=[a2_out[0]],
    )
    dx_send, wq_chip, *rest = tie(
        [dx_send, wq_chip] + list(a2_top[1:]), [array for array, _ in g_pieces]
    )
    a2_top = [a2_top[0]] + list(rest)

    near = (dx_keep + other_core(dx_send).astype(F32)).astype(BF)
    got = other_chip(near)
    if staged:
        z = [ent]
        z_next = hop(ent, n_ctx, top)
    wq_parts = [query_weight, other_core(query_weight), wq_chip, other_core(wq_chip)]
    hidden_grad, att_near, misc = simple(
        back_kernel,
        "back",
        [((half, width), F32), ((half, width), BF), ((16, width), F32)],
        core_arr,
        near,
        got,
        hidden_one,
        a2_mine,
        gates,
        ids,
        router,
        gain_two,
        cotangent,
        first=[wq_parts[1], wq_parts[3]],
    )
    att_far = other_core(att_near)
    (mix_send,) = tie([mix_send], [got])
    mix_near = (mix_keep + other_core(mix_send).astype(F32)).astype(BF)
    mix_got = other_chip(mix_near)
    a2_pieces = exchange_rest(a2_top, n_ctx, digits)
    if staged:
        (z_next,) = tie([z_next], [att_near])
        z.append(z_next)
        z_next = hop(z[1], n_ctx, top)

    begin = [att_near, att_far, output_weight, heads_f32]
    sides = [[kv_list[i] for i, k in enumerate(keys) if k[0] == r] for r in range(side)]
    dkv_far, head_grad, delta, dq_going = attend_back(
        q,
        kv_list[0],
        lse,
        [block for r in range(1, side) for block in sides[r]],
        heads,
        groups,
        start=begin,
        end=False,
        first=[mix_near] + ([z[1]] if staged else []),
    )
    (mix_got,) = tie([mix_got], [dq_going])
    dkv_far_got = hop(dkv_far, n_ctx, low)
    ids_all = routes(sides[0], tok, [dq_going])
    a2_stack, a2_stack_far = swapped(a2_pieces, [dq_going])
    g_stack, g_stack_far = swapped(g_pieces, [dq_going])
    terms_o = weight_terms(
        owner_turned,
        [([att_near, att_far], [heads_near, heads_far])],
        misc,
        first=[dq_going, a2_stack, g_stack],
    )
    kv_weight, mix_got = tie([kv_weight, mix_got], [])
    kv_chip = other_chip(kv_weight)
    waits = [ids_all, a2_stack_far, g_stack_far, terms_o]
    if staged:
        (z_next,) = tie([z_next], [terms_o])
        z.append(z_next)
        z_next = hop(z[2], n_ctx, top)
        waits = waits + [z[2]]
    o_sides = cut(terms_o, side)
    o_got = hop(o_sides[1], n_ctx, low)
    dkv_near, dq_near, dq_far = attend_back(
        q,
        kv_list[0],
        lse,
        sides[0],
        heads,
        groups,
        going=[head_grad, delta, dq_going],
        first=waits,
    )
    dkv_far_got, kv_chip = tie([dkv_far_got, kv_chip], [dq_near])
    kv_weights = [kv_weight, kv_core, kv_chip, other_core(kv_chip)]


    dkv_sides = [
        total([dkv_far_got[i : i + 1], dkv_near[i : i + 1]]).astype(BF)
        for i in range(dkv_near.shape[0])
    ]
    if staged:
        dkv_sent = scatter_sends(dkv_sides, n_ctx, top)
    dq_core = other_core(dq_far)

    terms_q = weight_terms(
        owner_turned,
        [([a1], [jnp.concatenate([dq_near, dq_far], axis=0)])],
        first=[dkv_sides[1 % len(dkv_sides)]],
    )
    dq_core, o_got = tie([dq_core, o_got], [terms_q, kv_weights[3]])
    dq_pair = jnp.stack([dq_near, dq_core], axis=0)
    q_sides = cut(terms_q, side)
    q_got = hop(q_sides[1], n_ctx, low)

    if staged:
        z_next, dq_pair = tie([z_next, dq_pair], [terms_q])
        z.append(z_next)
        ents = z
    else:
        upper = gather_ctx(ent, n_ctx, digits, upper_first[:-1])
        ents = [upper[k] for k in keys if k[0] == 0]
    dq_chip = other_chip(dq_pair)
    some = experts // 2
    places = tuple(range(len(ents)))
    shared = [a2_stack, a2_stack_far, g_stack, g_stack_far, ents]
    *grads_a, send_a = expert_grads(0, some, ids_all, places, *shared)
    (q_got,) = tie([q_got], [send_a])
    got_a = hop(send_a, n_ctx, low)
    (dq_chip,) = tie([dq_chip], [send_a])
    (query_back,) = simple(
        query_back_kernel,
        "query_back",
        [((half, width), F32)],
        core_arr,
        dq_pair,
        dq_chip,
        *wq_parts,
    )
    if staged:
        more = tie(dkv_sent[1:], [query_back])
        dkv_own = total([dkv_sent[0]] + list(more))[0].astype(BF)
    else:
        dkv_own = scatter_ctx(jnp.concatenate(dkv_sides, axis=0), n_ctx, digits[1:]).astype(BF)

    terms = jnp.concatenate(
        [total([o_sides[0], o_got]), total([q_sides[0], q_got])], axis=2
    ).astype(BF)
    dkv_parts = all_parts(dkv_own[:half], dkv_own[half:])
    late = weight_terms(owner_from, [([a1], [dkv_own])])
    *grads_b, send_b = expert_grads(
        some,
        experts - some,
        ids_all,
        places,
        *shared,
        first=[send_a, dkv_own, terms, late],
    )
    got_b = hop(send_b, n_ctx, low)
    *dkv_rest, got_a = tie(dkv_parts[1:] + [got_a], [send_b])
    dkv_parts = [dkv_parts[0]] + dkv_rest
    in_mine, norm_row = simple(
        input_kernel,
        "input",
        [((half, width), F32), ((8, width), F32)],
        core_arr,
        layer_input,
        gain_one,
        hidden_grad,
        query_back,
        *dkv_parts,
        *kv_weights,
    )
    in_far = other_core(in_mine)
    done = finish(0, experts, grads_a, got_a, first=[norm_row])
    late, mix_got = tie([late, mix_got], [send_b])
    out_mine = hidden_one + mix_near.astype(F32) + mix_got.astype(F32)
    out_far = other_core(out_mine)
    (layer_output,) = simple(
        place_kernel, "place", [((tok, width), F32)], core_arr, out_mine, out_far
    )
    (input_grad,) = simple(
        place_kernel, "place", [((tok, width), F32)], core_arr, in_mine, in_far
    )
    if staged:
        blocks = cut(terms, tops)
        moving = blocks[1]
        waits = [[send_b], [done[0]], [layer_output]]
        for r in range(2, tops + 1):
            (moving,) = tie([hop(moving, n_ctx, top)], waits[r - 2])
            moving = total([moving, blocks[r % tops]]).astype(BF if r < tops else F32)
        terms_own = moving[0]
    else:
        terms_own = scatter_ctx(terms, n_ctx, digits[1:])
    late_own = scatter_ctx(
        late, n_ctx, digits, lambda at, xs: tie(xs, [done[0]] if at else [layer_output, input_grad])
    )
    norm_rel = norm_row[0].reshape(n_ctx, cols)[owner_from]
    norm_own = scatter_ctx(norm_rel, n_ctx, digits, kind=F32)
    down_grad, gate_grad, up_grad = finish(some, experts, grads_b, got_b, done)

    qw = heads * HD
    output_grad = terms_own[:, :qw].T
    small = jnp.concatenate(
        [terms_own[:, qw : qw + experts + 1], norm_own[:, None]], axis=1
    )
    small = small + other_core(small)
    return (
        layer_output,
        input_grad,
        small[:, experts + 1],
        terms_own[:, qw + 128 :],
        late_own[:, :kvw],
        late_own[:, kvw:],
        output_grad,
        small[:, experts],
        small[:, :experts],
        gate_grad,
        up_grad,
        jnp.swapaxes(down_grad, 1, 2),
    )


def solution(mesh):
    in_specs = (
        P("ctx", None),
        P("ctx"),
        P("ctx", None),
        P(),
        P(None, "wa"),
        P(None, "wa"),
        P(None, "wa"),
        P("wa", None),
        P(),
        P(),
        P(None, None, "wa"),
        P(None, None, "wa"),
        P(None, "wa", None),
        P("ctx", None),
    )
    out_specs = (
        P("ctx", None),
        P("ctx", None),
        P("ctx"),
        P("ctx", "wa"),
        P("ctx", "wa"),
        P("ctx", "wa"),
        P("wa", "ctx"),
        P("ctx"),
        P("ctx", None),
        P(None, "ctx", "wa"),
        P(None, "ctx", "wa"),
        P(None, "wa", "ctx"),
    )
    return jax.shard_map(
        functools.partial(per_device, mesh.shape["ctx"]),
        mesh=mesh,
        in_specs=in_specs,
        out_specs=out_specs,
        check_vma=False,
    )
```

profile of v0, /device:TPU:0, one launch (start us, length us, event | category | flops | bytes accessed | tf_op | source)
XLA Modules:
  0.0 371.6 jit_solution(14056080026061527243)
XLA Ops:
  4.7 5.0 %project.1 = (bf16[512,1536]{1,0:T(8,128)(2,1)}, bf16[512,384]{1,0:T(8,128)(2,1)}, bf16[528,256]{1,0:T(8,128)(2,1)}) custom-call(s32[1]{0:T(128)} %bitcast.core_ref.refs_0_, bf16[512,1536]{1,0:T(8,128)(2,1)} %x_ref.7, f32[1536]{0:T(1024)} %gain_ref.5, bf16[1536,384]{1,0:T(8,128)(2,1)} %refs_2_.1, bf16[1536,128]{1,0:T(8,128)(2,1)} %wk_ref.1, ...), custom_call_target="tpu_custom_call" | custom-call | flops 1500000000 | bytes 4500000 | tf_op jit(solution)/shard_map/project/pallas_call | solution.py:241
  14.5 4.8 %collective-permute-done.1.refs_1_ = bf16[528,256]{1,0:T(8,128)(2,1)S(1)} collective-permute-done((bf16[528,256]{1,0:T(8,128)(2,1)}, bf16[528,256]{1,0:T(8,128)(2,1)S(1)}, u32[]{:S(2)}, u32[]{:S(2)}) %collective-permute-start.1) | collective-permute-done | bytes 270368 | tf_op jit(solution)/shard_map/ppermute | solution.py:49
  24.1 6.7 %collective-permute-done.3.refs_1_ = bf16[528,256]{1,0:T(8,128)(2,1)S(1)} collective-permute-done((bf16[528,256]{1,0:T(8,128)(2,1)}, bf16[528,256]{1,0:T(8,128)(2,1)S(1)}, u32[]{:S(2)}, u32[]{:S(2)}) %collective-permute-start.3) | collective-permute-done | bytes 270368 | tf_op jit(solution)/shard_map/ppermute | solution.py:49
  45.8 5.1 %collective-permute-done.7.refs_8_.refs_6_ = bf16[528,256]{1,0:T(8,128)(2,1)S(1)} collective-permute-done((bf16[528,256]{1,0:T(8,128)(2,1)}, bf16[528,256]{1,0:T(8,128)(2,1)S(1)}, u32[]{:S(2)}, u32[]{:S(2)}) %collective-permute-start.7) | collective-permute-done | bytes 270368 | tf_op jit(solution)/shard_map/ppermute | solution.py:49
  51.7 22.2 %attend.1 = (f32[512,384]{1,0:T(8,128)}, bf16[256,384]{1,0:T(8,128)(2,1)}, bf16[256,384]{1,0:T(8,128)(2,1)}, f32[8,512]{1,0:T(8,128)}) custom-call(bf16[512,384]{1,0:T(8,128)(2,1)} %get-tuple-element.106.refs_0_, bf16[528,256]{1,0:T(8,128)(2,1)} %get-tuple-element.107.refs_0_.refs_1_.refs_3_, bf16[528,256]{1,0:T(8,128)(2,1)} %get-tuple-element.108.refs_2_.refs_3_, ...), custom_call_target="tpu_custom_call" | custom-call | flops 8099999744 | bytes 24300000 | tf_op jit(solution)/shard_map/attend/pallas_call | solution.py:401
  77.2 5.8 %collective-permute-done.13.refs_2_ = bf16[256,384]{1,0:T(8,128)(2,1)S(1)} collective-permute-done((bf16[256,384]{1,0:T(8,128)(2,1)}, bf16[256,384]{1,0:T(8,128)(2,1)S(1)}, u32[]{:S(2)}, u32[]{:S(2)}) %collective-permute-start.13) | collective-permute-done | bytes 196640 | tf_op jit(solution)/shard_map/ppermute | solution.py:57
  88.2 6.3 %middle.1 = (f32[256,1536]{1,0:T(8,128)}, bf16[256,1536]{1,0:T(8,128)(2,1)}) custom-call(s32[1]{0:T(128)} %bitcast.core_ref.refs_0_, bf16[512,1536]{1,0:T(8,128)(2,1)} %x_ref.7, f32[1536]{0:T(1024)} %refs_8_.3, bf16[256,384]{1,0:T(8,128)(2,1)} %get-tuple-element.120.refs_0_.refs_3_, bf16[256,384]{1,0:T(8,128)(2,1)} %copy-done.42, ...), custom_call_target="tpu_custom_call" | custom-call | flops 1500000000 | bytes 4500000 | tf_op jit(solution)/shard_map/middle/pallas_call | solution.py:811
  103.8 32.1 %experts.1 = (f32[256,1536]{1,0:T(8,128)}, bf16[256,1536]{1,0:T(8,128)(2,1)}, f32[256,1664]{1,0:T(8,128)}, bf16[256,1664]{1,0:T(8,128)(2,1)}, f32[512,8]{1,0:T(8,128)}, /*index=5*/bf16[6,512,256]{2,1,0:T(8,128)(2,1)}) custom-call(s32[1]{0:T(128)} %bitcast.core_ref.refs_0_, s32[512,2]{1,0:T(8,128)} %get-tuple-element.227.refs_1_.refs_6_, ...), custom_call_target="tpu_custom_call" | custom-call | flops 9600000000 | bytes 28800000 | tf_op jit(solution)/shard_map/experts/pallas_call | solution.py:684
  142.8 19.4 %collective-permute-done.23.refs_1_.refs_2_ = bf16[256,1664]{1,0:T(8,128)(2,1)} collective-permute-done((bf16[256,1664]{1,0:T(8,128)(2,1)S(1)}, bf16[256,1664]{1,0:T(8,128)(2,1)}, u32[]{:S(2)}, u32[]{:S(2)}) %collective-permute-start.23) | collective-permute-done | bytes 852000 | tf_op jit(solution)/shard_map/ppermute | solution.py:57
  162.3 5.6 %back.1 = (f32[256,1536]{1,0:T(8,128)}, bf16[256,1536]{1,0:T(8,128)(2,1)}, f32[16,1536]{1,0:T(8,128)}) custom-call(s32[1]{0:T(128)} %bitcast.core_ref.refs_0_, bf16[256,1664]{1,0:T(8,128)(2,1)} %copy-done.11, bf16[256,1664]{1,0:T(8,128)(2,1)} %collective-permute-done.23.refs_1_.refs_2_, f32[256,1536]{1,0:T(8,128)} %get-tuple-element.123.refs_3_, ...), custom_call_target="tpu_custom_call" | custom-call | flops 1500000000 | bytes 4500000 | tf_op jit(solution)/shard_map/back/pallas_call | solution.py:811
  168.3 11.4 %collective-permute-done.28.refs_0_ = bf16[6,512,256]{2,1,0:T(8,128)(2,1)S(1)} collective-permute-done((bf16[6,512,256]{2,1,0:T(8,128)(2,1)S(1)}, bf16[6,512,256]{2,1,0:T(8,128)(2,1)S(1)}, u32[]{:S(2)}, u32[]{:S(2)}) %collective-permute-start.28) | collective-permute-done | bytes 1572896 | tf_op jit(solution)/shard_map/ppermute | solution.py:49
  184.4 19.5 %attend_back.2 = (bf16[4,512,256]{2,1,0:T(8,128)(2,1)}, bf16[512,384]{1,0:T(8,128)(2,1)}, f32[8,512]{1,0:T(8,128)}, f32[4,64,768]{2,1,0:T(8,128)}) custom-call(bf16[512,384]{1,0:T(8,128)(2,1)} %get-tuple-element.106.refs_0_, bf16[528,256]{1,0:T(8,128)(2,1)} %get-tuple-element.107.refs_0_.refs_1_.refs_3_, f32[8,512]{1,0:T(8,128)} %get-tuple-element.138.refs_2_, ...), custom_call_target="tpu_custom_call" | custom-call | flops 5400000000 | bytes 16200000 | tf_op jit(solution)/shard_map/attend_back/pallas_call | solution.py:530
  211.0 4.1 %weight_terms.3.refs_1_.refs_13_ = bf16[8,192,512]{2,1,0:T(8,128)(2,1)} custom-call(s32[8]{0:T(128)} %stack.107.refs_0_, bf16[256,1536]{1,0:T(8,128)(2,1)} %get-tuple-element.141.refs_1_.refs_7_, bf16[256,1536]{1,0:T(8,128)(2,1)} %collective-permute-done.27.refs_8_.refs_2_, bf16[256,384]{1,0:T(8,128)(2,1)} %get-tuple-element.120.refs_0_.refs_3_, ...), custom_call_target="tpu_custom_call" | custom-call | flops 1200000000 | bytes 3600000 | tf_op jit(solution)/shard_map/weight_terms/pallas_call | solution.py:978
  223.2 17.9 %attend_back.3 = (bf16[4,512,256]{2,1,0:T(8,128)(2,1)}, bf16[256,384]{1,0:T(8,128)(2,1)}, bf16[256,384]{1,0:T(8,128)(2,1)}) custom-call(bf16[512,384]{1,0:T(8,128)(2,1)} %get-tuple-element.106.refs_0_, bf16[528,256]{1,0:T(8,128)(2,1)} %get-tuple-element.107.refs_0_.refs_1_.refs_3_, f32[8,512]{1,0:T(8,128)} %get-tuple-element.138.refs_2_, ...), custom_call_target="tpu_custom_call" | custom-call | flops 5400000000 | bytes 16200000 | tf_op jit(solution)/shard_map/attend_back/pallas_call | solution.py:530
  246.0 3.9 %weight_terms.4.refs_2_ = bf16[8,192,384]{2,1,0:T(8,128)(2,1)} custom-call(s32[8]{0:T(128)} %stack.107.refs_0_, bf16[512,1536]{1,0:T(8,128)(2,1)} %get-tuple-element.137.refs_1_.refs_0_, bf16[512,384]{1,0:T(8,128)(2,1)} %pad_maximum_fusion.1.refs_2_, bf16[1,512,256]{2,1,0:T(8,128)(2,1)} %get-tuple-element.230.refs_3_), custom_call_target="tpu_custom_call" | custom-call | flops 1200000000 | bytes 3600000 | tf_op jit(solution)/shard_map/weight_terms/pallas_call | solution.py:978
  261.8 12.0 %expert_grads.2 = (f32[4,192,256]{2,1,0:T(8,128)}, f32[4,192,256]{2,1,0:T(8,128)}, f32[4,192,256]{2,1,0:T(8,128)}, bf16[3,4,192,256]{3,2,1,0:T(8,128)(2,1)}) custom-call(f32[4,512,8]{2,1,0:T(8,128)} %routes.1.refs_10_.ids_ref.refs_0_, bf16[4,384,256]{2,1,0:T(8,128)(2,1)} %stacked.2.refs_7_.refs_0_.refs_1_, ...), custom_call_target="tpu_custom_call" | custom-call | flops 1440000000 | bytes 4320000 | tf_op jit(solution)/shard_map/expert_grads/pallas_call | solution.py:763
  280.6 5.5 %query_back.1.refs_3_.query_ref = f32[256,1536]{1,0:T(8,128)} custom-call(s32[1]{0:T(128)} %bitcast.core_ref.refs_0_, bf16[2,256,384]{2,1,0:T(8,128)(2,1)} %get-tuple-element.167.refs_0_, bf16[2,256,384]{2,1,0:T(8,128)(2,1)} %tie.40.refs_1_, bf16[1536,384]{1,0:T(8,128)(2,1)} %refs_2_.1, bf16[1536,384]{1,0:T(8,128)(2,1)} %collective-permute-done.25.refs_10_.refs_3_, ...), custom_call_target="tpu_custom_call" | custom-call | flops 1500000000 | bytes 4500000 | tf_op jit(solution)/shard_map/query_back/pallas_call | solution.py:811
  292.4 11.8 %expert_grads.3 = (f32[4,192,256]{2,1,0:T(8,128)}, f32[4,192,256]{2,1,0:T(8,128)}, f32[4,192,256]{2,1,0:T(8,128)}, bf16[3,4,192,256]{3,2,1,0:T(8,128)(2,1)}) custom-call(f32[4,512,8]{2,1,0:T(8,128)} %routes.1.refs_10_.ids_ref.refs_0_, bf16[4,384,256]{2,1,0:T(8,128)(2,1)} %stacked.2.refs_7_.refs_0_.refs_1_, ...), custom_call_target="tpu_custom_call" | custom-call | flops 1440000000 | bytes 4320000 | tf_op jit(solution)/shard_map/expert_grads/pallas_call | solution.py:763
  318.5 6.1 %input.1 = (f32[256,1536]{1,0:T(8,128)}, f32[8,1536]{1,0:T(8,128)}) custom-call(s32[1]{0:T(128)} %bitcast.core_ref.refs_0_, bf16[512,1536]{1,0:T(8,128)(2,1)} %x_ref.7, f32[1536]{0:T(1024)} %gain_ref.5, f32[256,1536]{1,0:T(8,128)} %get-tuple-element.177.grad_ref, f32[256,1536]{1,0:T(8,128)} %query_back.1.refs_3_.query_ref, bf16[256,256]{1,0:T(8,128)(2,1)} %copy-done.34, ...), custom_call_target="tpu_custom_call" | custom-call | flops 1500000000 | bytes 4500000 | tf_op jit(solution)/shard_map/input/pallas_call | solution.py:811
  325.5 4.2 %finish.2 = (f32[8,192,256]{2,1,0:T(8,128)}, f32[8,192,256]{2,1,0:T(8,128)}, f32[8,192,256]{2,1,0:T(8,128)}) custom-call(f32[4,192,256]{2,1,0:T(8,128)} %get-tuple-element.182.refs_0_, f32[4,192,256]{2,1,0:T(8,128)} %get-tuple-element.183.refs_1_, f32[4,192,256]{2,1,0:T(8,128)} %get-tuple-element.184.refs_2_, ...), custom_call_target="tpu_custom_call" | custom-call | flops 900000000 | bytes 2700000 | tf_op jit(solution)/shard_map/finish/pallas_call | solution.py:790
  331.9 6.6 %collective-permute-done.59.refs_1_ = bf16[2,192,256]{2,1,0:T(8,128)(2,1)} collective-permute-done((bf16[2,192,256]{2,1,0:T(8,128)(2,1)}, bf16[2,192,256]{2,1,0:T(8,128)(2,1)}, u32[]{:S(2)}, u32[]{:S(2)}) %collective-permute-start.59) | collective-permute-done | bytes 196640 | tf_op jit(solution)/shard_map/ppermute | solution.py:49
  338.4 4.0 %collective-permute-start.53 = (f32[2,192]{1,0:T(2,128)S(1)}, f32[2,192]{1,0:T(2,128)S(1)}, u32[]{:S(2)}, u32[]{:S(2)}) collective-permute-start(f32[2,192]{1,0:T(2,128)S(1)} %get-tuple-element.242), channel_id=1, source_target_pairs={{0,24},{4,28},{8,0},{12,4},{16,8},{20,12},{24,16},{28,20},{1,25},{... | collective-permute-start | bytes 4616 | tf_op jit(solution)/shard_map/ppermute | solution.py:49
  352.4 4.2 %finish.3 = (f32[8,192,256]{2,1,0:T(8,128)}, f32[8,192,256]{2,1,0:T(8,128)}, f32[8,192,256]{2,1,0:T(8,128)}) custom-call(f32[4,192,256]{2,1,0:T(8,128)} %get-tuple-element.192.refs_0_, f32[4,192,256]{2,1,0:T(8,128)} %get-tuple-element.193.refs_1_, ...), custom_call_target="tpu_custom_call", output_to_operand_aliasing={{0}: (4, {}), {1}: (5, {}), {2}: (6, {})} | custom-call | flops 900000000 | bytes 2700000 | tf_op jit(solution)/shard_map/finish/pallas_call | solution.py:790
  365.8 3.8 %place.3.refs_2_ = f32[512,1536]{1,0:T(8,128)} custom-call(s32[1]{0:T(128)} %bitcast.core_ref.refs_0_, f32[256,1536]{1,0:T(8,128)} %get-tuple-element.181.mine_ref, f32[256,1536]{1,0:T(8,128)} %collective-permute-done.49.theirs_ref), custom_call_target="tpu_custom_call" | custom-call | flops 1500000000 | bytes 4500000 | tf_op jit(solution)/shard_map/place/pallas_call | solution.py:811
  (298 shorter events, 141.9 us)
Async XLA Ops:
  35.1 38.9 %collective-permute-start.8 = (bf16[384,1536]{1,0:T(8,128)(2,1)}, bf16[384,1536]{1,0:T(8,128)(2,1)S(1)}, u32[]{:S(2)}, u32[]{:S(2)}) collective-permute-start(bf16[384,1536]{1,0:T(8,128)(2,1)} %refs_9_.3), channel_id=1, source_target_pairs={{0,2},{1,3},{2,0},{3,1},{4,6},{5,7},{6,4},{7,5},{8,10},{9,11},{10,... | collective-permute-start | bytes 3538952 | tf_op jit(solution)/shard_map/ppermute | solution.py:57
  45.0 32.3 %collective-permute-start.15 = (bf16[384,1536]{1,0:T(8,128)(2,1)}, bf16[384,1536]{1,0:T(8,128)(2,1)S(1)}, u32[]{:S(2)}, u32[]{:S(2)}) collective-permute-start(bf16[384,1536]{1,0:T(8,128)(2,1)} %refs_9_.3), channel_id=1, source_target_pairs={{0,1},{1,0},{2,3},{3,2},{4,5},{5,4},{6,7},{7,6},{8,9},{9,8},{10,11... | collective-permute-start | bytes 3538952 | tf_op jit(solution)/shard_map/ppermute | solution.py:53
  45.0 28.9 %collective-permute-start.9 = (bf16[1,384,256]{2,1,0:T(8,128)(2,1)}, bf16[1,384,256]{2,1,0:T(8,128)(2,1)S(1)}, u32[]{:S(2)}, u32[]{:S(2)}) collective-permute-start(bf16[1,384,256]{2,1,0:T(8,128)(2,1)} %get-tuple-element.117), channel_id=1, source_target_pairs={{0,8},{4,12},{8,16},{12,20},{16,24},{20,28},{24,0},{28,4},{1,9},{5... | collective-permute-start | bytes 589832 | tf_op jit(solution)/shard_map/ppermute | solution.py:49
  45.0 28.9 %collective-permute-start.10 = (bf16[1,384,256]{2,1,0:T(8,128)(2,1)}, bf16[1,384,256]{2,1,0:T(8,128)(2,1)S(1)}, u32[]{:S(2)}, u32[]{:S(2)}) collective-permute-start(bf16[1,384,256]{2,1,0:T(8,128)(2,1)} %get-tuple-element.118), channel_id=1, source_target_pairs={{0,16},{4,20},{8,24},{12,28},{16,0},{20,4},{24,8},{28,12},{1,17},{... | collective-permute-start | bytes 589832 | tf_op jit(solution)/shard_map/ppermute | solution.py:49
  94.8 41.1 %collective-permute-start.18 = (bf16[1536,384]{1,0:T(8,128)(2,1)}, bf16[1536,384]{1,0:T(8,128)(2,1)}, u32[]{:S(2)}, u32[]{:S(2)}) collective-permute-start(bf16[1536,384]{1,0:T(8,128)(2,1)} %refs_2_.1), channel_id=1, source_target_pairs={{0,2},{1,3},{2,0},{3,1},{4,6},{5,7},{6,4},{7,5},{8,10},{9,11},{10,... | collective-permute-start | bytes 3538952 | tf_op jit(solution)/shard_map/ppermute | solution.py:57
  98.6 37.3 %collective-permute-start.19 = (bf16[1,384,256]{2,1,0:T(8,128)(2,1)}, bf16[1,384,256]{2,1,0:T(8,128)(2,1)S(1)}, u32[]{:S(2)}, u32[]{:S(2)}) collective-permute-start(bf16[1,384,256]{2,1,0:T(8,128)(2,1)} %get-tuple-element.130), channel_id=1, source_target_pairs={{0,8},{4,12},{8,16},{12,20},{16,24},{20,28},{24,0},{28,4},{1,9},{5... | collective-permute-start | bytes 589832 | tf_op jit(solution)/shard_map/ppermute | solution.py:49
  99.3 36.7 %collective-permute-start.20 = (bf16[1,384,256]{2,1,0:T(8,128)(2,1)}, bf16[1,384,256]{2,1,0:T(8,128)(2,1)S(1)}, u32[]{:S(2)}, u32[]{:S(2)}) collective-permute-start(bf16[1,384,256]{2,1,0:T(8,128)(2,1)} %get-tuple-element.131), channel_id=1, source_target_pairs={{0,16},{4,20},{8,24},{12,28},{16,0},{20,4},{24,8},{28,12},{1,17},{... | collective-permute-start | bytes 589832 | tf_op jit(solution)/shard_map/ppermute | solution.py:49
  99.3 36.7 %collective-permute-start.21 = (bf16[1,384,256]{2,1,0:T(8,128)(2,1)}, bf16[1,384,256]{2,1,0:T(8,128)(2,1)S(1)}, u32[]{:S(2)}, u32[]{:S(2)}) collective-permute-start(bf16[1,384,256]{2,1,0:T(8,128)(2,1)} %get-tuple-element.132), channel_id=1, source_target_pairs={{0,24},{4,28},{8,0},{12,4},{16,8},{20,12},{24,16},{28,20},{1,25},{... | collective-permute-start | bytes 589832 | tf_op jit(solution)/shard_map/ppermute | solution.py:49
  141.7 38.0 %collective-permute-start.28 = (bf16[6,512,256]{2,1,0:T(8,128)(2,1)S(1)}, bf16[6,512,256]{2,1,0:T(8,128)(2,1)S(1)}, u32[]{:S(2)}, u32[]{:S(2)}) collective-permute-start(bf16[6,512,256]{2,1,0:T(8,128)(2,1)S(1)} %copy-done.8), channel_id=1, source_target_pairs={{0,8},{4,12},{8,16},{12,20},{16,24},{20,28},{24,0},{28,4},{1,9},{5... | collective-permute-start | bytes 4718600 | tf_op jit(solution)/shard_map/ppermute | solution.py:49
  180.8 37.4 %collective-permute-start.34 = (bf16[6,512,256]{2,1,0:T(8,128)(2,1)}, bf16[6,512,256]{2,1,0:T(8,128)(2,1)S(1)}, u32[]{:S(2)}, u32[]{:S(2)}) collective-permute-start(bf16[6,512,256]{2,1,0:T(8,128)(2,1)} %tie.31.refs_12_.refs_5_.refs_6_), channel_id=1, source_target_pairs={{0,8},{4,12},{8,16},{12,20},{16,24},{20,28},{24,0},{28,4},{1,9},{5... | collective-permute-start | bytes 4718600 | tf_op jit(solution)/shard_map/ppermute | solution.py:49
  182.8 25.9 %collective-permute-start.30 = (bf16[256,1536]{1,0:T(8,128)(2,1)S(1)}, bf16[256,1536]{1,0:T(8,128)(2,1)S(1)}, u32[]{:S(2)}, u32[]{:S(2)}) collective-permute-start(bf16[256,1536]{1,0:T(8,128)(2,1)S(1)} %add_convert_fusion.2.refs_11_), channel_id=1, source_target_pairs={{0,2},{1,3},{2,0},{3,1},{4,6},{5,7},{6,4},{7,5},{8,10},{9,11},{10,... | collective-permute-start | bytes 2359304 | tf_op jit(solution)/shard_map/ppermute | solution.py:57
  208.7 32.4 %collective-permute-start.29 = (bf16[4,512,256]{2,1,0:T(8,128)(2,1)}, bf16[4,512,256]{2,1,0:T(8,128)(2,1)}, u32[]{:S(2)}, u32[]{:S(2)}) collective-permute-start(bf16[4,512,256]{2,1,0:T(8,128)(2,1)} %get-tuple-element.144), channel_id=1, source_target_pairs={{0,4},{4,0},{8,12},{12,8},{16,20},{20,16},{24,28},{28,24},{1,5},{5... | collective-permute-start | bytes 3145736 | tf_op jit(solution)/shard_map/ppermute | solution.py:49
  209.6 31.5 %collective-permute-start.31 = (bf16[1536,256]{1,0:T(8,128)(2,1)}, bf16[1536,256]{1,0:T(8,128)(2,1)}, u32[]{:S(2)}, u32[]{:S(2)}) collective-permute-start(bf16[1536,256]{1,0:T(8,128)(2,1)} %get-tuple-element.146.refs_4_), channel_id=1, source_target_pairs={{0,2},{1,3},{2,0},{3,1},{4,6},{5,7},{6,4},{7,5},{8,10},{9,11},{10,... | collective-permute-start | bytes 2359304 | tf_op jit(solution)/shard_map/ppermute | solution.py:57
  219.5 39.7 %collective-permute-start.38 = (bf16[6,512,256]{2,1,0:T(8,128)(2,1)}, bf16[6,512,256]{2,1,0:T(8,128)(2,1)S(1)}, u32[]{:S(2)}, u32[]{:S(2)}) collective-permute-start(bf16[6,512,256]{2,1,0:T(8,128)(2,1)} %tie.36.refs_14_.refs_6_.refs_7_), channel_id=1, source_target_pairs={{0,8},{4,12},{8,16},{12,20},{16,24},{20,28},{24,0},{28,4},{1,9},{5... | collective-permute-start | bytes 4718600 | tf_op jit(solution)/shard_map/ppermute | solution.py:49
  223.2 30.9 %collective-permute-start.40 = (bf16[4,192,512]{2,1,0:T(8,128)(2,1)}, bf16[4,192,512]{2,1,0:T(8,128)(2,1)S(1)}, u32[]{:S(2)}, u32[]{:S(2)}) collective-permute-start(bf16[4,192,512]{2,1,0:T(8,128)(2,1)} %slice.194), channel_id=1, source_target_pairs={{0,4},{4,0},{8,12},{12,8},{16,20},{20,16},{24,28},{28,24},{1,5},{5... | collective-permute-start | bytes 2359304 | tf_op jit(solution)/shard_map/ppermute | solution.py:49
  254.1 32.1 %collective-permute-start.35 = (bf16[1,512,256]{2,1,0:T(8,128)(2,1)}, bf16[1,512,256]{2,1,0:T(8,128)(2,1)}, u32[]{:S(2)}, u32[]{:S(2)}) collective-permute-start(bf16[1,512,256]{2,1,0:T(8,128)(2,1)} %get-tuple-element.230.refs_3_), channel_id=1, source_target_pairs={{0,24},{4,28},{8,0},{12,4},{16,8},{20,12},{24,16},{28,20},{1,25},{... | collective-permute-start | bytes 786440 | tf_op jit(solution)/shard_map/ppermute | solution.py:49
  254.3 31.9 %collective-permute-start.37 = (bf16[1,512,256]{2,1,0:T(8,128)(2,1)}, bf16[1,512,256]{2,1,0:T(8,128)(2,1)}, u32[]{:S(2)}, u32[]{:S(2)}) collective-permute-start(bf16[1,512,256]{2,1,0:T(8,128)(2,1)} %get-tuple-element.228), channel_id=1, source_target_pairs={{0,8},{4,12},{8,16},{12,20},{16,24},{20,28},{24,0},{28,4},{1,9},{5... | collective-permute-start | bytes 786440 | tf_op jit(solution)/shard_map/ppermute | solution.py:49
  256.3 29.8 %collective-permute-start.36 = (bf16[1,512,256]{2,1,0:T(8,128)(2,1)}, bf16[1,512,256]{2,1,0:T(8,128)(2,1)}, u32[]{:S(2)}, u32[]{:S(2)}) collective-permute-start(bf16[1,512,256]{2,1,0:T(8,128)(2,1)} %get-tuple-element.229), channel_id=1, source_target_pairs={{0,16},{4,20},{8,24},{12,28},{16,0},{20,4},{24,8},{28,12},{1,17},{... | collective-permute-start | bytes 786440 | tf_op jit(solution)/shard_map/ppermute | solution.py:49
  275.4 43.1 %collective-permute-start.48 = (bf16[3,4,192,256]{3,2,1,0:T(8,128)(2,1)S(1)}, bf16[3,4,192,256]{3,2,1,0:T(8,128)(2,1)}, u32[]{:S(2)}, u32[]{:S(2)}) collective-permute-start(bf16[3,4,192,256]{3,2,1,0:T(8,128)(2,1)S(1)} %copy-done.7), channel_id=1, source_target_pairs={{0,4},{4,0},{8,12},{12,8},{16,20},{20,16},{24,28},{28,24},{1,5},{5... | collective-permute-start | bytes 3538952 | tf_op jit(solution)/shard_map/ppermute | solution.py:49
  279.0 26.9 %collective-permute-start.50 = (bf16[1,192,896]{2,1,0:T(8,128)(2,1)}, bf16[1,192,896]{2,1,0:T(8,128)(2,1)}, u32[]{:S(2)}, u32[]{:S(2)}) collective-permute-start(bf16[1,192,896]{2,1,0:T(8,128)(2,1)} %fusion), channel_id=1, source_target_pairs={{0,8},{4,12},{8,16},{12,20},{16,24},{20,28},{24,0},{28,4},{1,9},{5... | collective-permute-start | bytes 1032200 | tf_op jit(solution)/shard_map/ppermute | solution.py:49
  288.4 26.6 %collective-permute-start.45 = (bf16[256,256]{1,0:T(8,128)(2,1)}, bf16[256,256]{1,0:T(8,128)(2,1)}, u32[]{:S(2)}, u32[]{:S(2)}) collective-permute-start(bf16[256,256]{1,0:T(8,128)(2,1)} %get-tuple-element.236), channel_id=1, source_target_pairs={{0,1},{1,0},{2,3},{3,2},{4,5},{5,4},{6,7},{7,6},{8,9},{9,8},{10,11... | collective-permute-start | bytes 393224 | tf_op jit(solution)/shard_map/ppermute | solution.py:53
  304.2 48.1 %collective-permute-start.62 = (bf16[3,4,192,256]{3,2,1,0:T(8,128)(2,1)}, bf16[3,4,192,256]{3,2,1,0:T(8,128)(2,1)}, u32[]{:S(2)}, u32[]{:S(2)}) collective-permute-start(bf16[3,4,192,256]{3,2,1,0:T(8,128)(2,1)} %get-tuple-element.175.refs_2_.refs_4_.refs_1_), channel_id=1, source_target_pairs={{0,4},{4,0},{8,12},{12,8},{16,20},{20,16},{24,28},{28,24},{1,5},{5... | collective-permute-start | bytes 3538952 | tf_op jit(solution)/shard_map/ppermute | solution.py:49
  314.1 29.0 %collective-permute-start.51 = (bf16[1,192,896]{2,1,0:T(8,128)(2,1)}, bf16[1,192,896]{2,1,0:T(8,128)(2,1)}, u32[]{:S(2)}, u32[]{:S(2)}) collective-permute-start(bf16[1,192,896]{2,1,0:T(8,128)(2,1)} %add_convert_fusion.5), channel_id=1, source_target_pairs={{0,8},{4,12},{8,16},{12,20},{16,24},{20,28},{24,0},{28,4},{1,9},{5... | collective-permute-start | bytes 1032200 | tf_op jit(solution)/shard_map/ppermute | solution.py:49
  318.5 38.1 %collective-permute-start.44 = (f32[256,1536]{1,0:T(8,128)}, f32[256,1536]{1,0:T(8,128)S(1)}, u32[]{:S(2)}, u32[]{:S(2)}) collective-permute-start(f32[256,1536]{1,0:T(8,128)} %convert_add_fusion.mine_ref), channel_id=1, source_target_pairs={{0,1},{1,0},{2,3},{3,2},{4,5},{5,4},{6,7},{7,6},{8,9},{9,8},{10,11... | collective-permute-start | bytes 4718600 | tf_op jit(solution)/shard_map/ppermute | solution.py:53
  (86 other events, 665.2 us)
where the time goes:
time: 378 us; the launch traced here: 372 us
  Pallas kernels  183 us (48%)
  waiting for transfers between devices  83.3 us (22%)
  starting transfers between devices  48.2 us (13%)
  local copies, waits for them, and re-layouts  30.1 us (8%)
  other arithmetic  25.4 us (7%)
    ppermute x35, waiting for transfers between devices, hop(): return lax.ppermute(x, 'ctx', moved(n, digit, shift))  51.7 us
    pallas_call x2, Pallas kernels, attend_back(): pl.pallas_call(drop_first(kernel, len(operands), len(first)), out_shape=t...  37.4 us
    ppermute x35, starting transfers between devices, hop(): return lax.ppermute(x, 'ctx', moved(n, digit, shift))  34 us
    pallas_call x1, Pallas kernels, experts_call(): pl.pallas_call(drop_first(experts_kernel, 9, len(first)), out_shape=(jax....  32.1 us
    pallas_call x6, Pallas kernels, simple(): pl.pallas_call(drop_first(kernel, 1 + len(operands), len(first)), out_sha...  31.1 us
    ppermute x8, waiting for transfers between devices, other_chip(): return lax.ppermute(x, 'wa', [(i, i ^ 2) for i in range(4)])  25.2 us
    pallas_call x2, Pallas kernels, expert_grads(): pl.pallas_call(drop_first(kernel, len(operands), len(first)), out_shape=(...  23.8 us
    pallas_call x1, Pallas kernels, attend(): pl.pallas_call(drop_first(functools.partial(attend_kernel, nb, heads, gro...  22.2 us
  transfers between devices with their start and end apart: 63, of which 18 were waited for; matrix products, arithmetic and copies ran while one was open for 9% of the time, Pallas kernels for 46%

commit v1 on v0

--- a/solution.py
+++ b/solution.py
@@ -574,7 +574,17 @@
     )(*blocks, *first)
 
 
+def masks(ids_ref, rows, e, count, width):
+    return [
+        jnp.broadcast_to(
+            jnp.where(ids_ref[rows, c : c + 1] == e, 1.0, 0.0).astype(BF), (count, width)
+        )
+        for c in range(2)
+    ]
+
+
 def experts_kernel(
+    per,
     core_ref,
     ids_ref,
     mine_ref,
@@ -584,19 +594,16 @@
     wg_ref,
     wu_ref,
     wd_ref,
-    mix_keep_ref,
-    mix_send_ref,
     dx_keep_ref,
     dx_send_ref,
     gates_ref,
     ent_ref,
     a2_s,
     g_s,
-    mix_s,
     dx_s,
     back_s,
 ):
-    e = pl.program_id(0)
+    step = pl.program_id(0)
     tok, width = a2_s.shape
     half = tok // 2
     experts = wr_ref.shape[0]
@@ -604,7 +611,7 @@
     first = ids_ref[:, 0:1]
     second = ids_ref[:, 1:2]
 
-    @pl.when(e == 0)
+    @pl.when(step == 0)
     def _():
         a2_s[:half, :] = mine_ref[...]
         a2_s[half:, :] = theirs_ref[...]
@@ -617,52 +624,59 @@
         top = jnp.maximum(one, two)
         one = jnp.exp(one - top)
         two = jnp.exp(two - top)
-        total = one + two
-        gates_ref[...] = jnp.where(lane == first, one / total, 0.0) + jnp.where(
-            lane == second, two / total, 0.0
+        both = one + two
+        gates_ref[...] = jnp.where(lane == first, one / both, 0.0) + jnp.where(
+            lane == second, two / both, 0.0
         )
-        mix_s[...] = jnp.zeros(mix_s.shape, F32)
         dx_s[...] = jnp.zeros(dx_s.shape, F32)
         back_s[...] = jnp.zeros(back_s.shape, F32)
         ent_ref[...] = jnp.zeros(ent_ref.shape, BF)
 
-    wg = wg_ref[0]
-    wu = wu_ref[0]
-    wd = wd_ref[0]
     for i in range(2):
         rows = pl.ds(i * half, half)
         a2 = a2_s[rows, :]
-        u = jnp.dot(a2, wg, preferred_element_type=F32)
-        w = jnp.dot(a2, wu, preferred_element_type=F32)
-        m = lax.dot_general(g_s[rows, :], wd, NT, preferred_element_type=F32)
-        here = lane[:half] == e
-        gate = jnp.sum(jnp.where(here, gates_ref[rows, :], 0.0), axis=1, keepdims=True)
-        pick_one = (ids_ref[rows, 0:1] == e).astype(F32)
-        pick_two = (ids_ref[rows, 1:2] == e).astype(F32)
-        sig = 1.0 / (1.0 + jnp.exp(-u))
-        act = u * sig
-        mid = (act * w).astype(BF).astype(F32)
-        back = jnp.sum(mid * m, axis=1, keepdims=True) * (pick_one + pick_two)
-        back_s[rows, :] += jnp.where(here, back, 0.0)
-        mid = mid * gate
-        gm = gate * m
-        up_back = gm * act
-        pre_back = gm * w * sig * (1.0 + u * (1.0 - sig))
-        mid_b = mid.astype(BF)
-        up_b = up_back.astype(BF)
-        pre_b = pre_back.astype(BF)
-        mix_s[rows, :] += jnp.dot(mid_b, wd, preferred_element_type=F32)
-        dx_s[rows, :] += lax.dot_general(
-            pre_b, wg, NT, preferred_element_type=F32
-        ) + lax.dot_general(up_b, wu, NT, preferred_element_type=F32)
-        for kind, value in enumerate((mid, pre_back, up_back)):
-            for c, pick in enumerate((pick_one, pick_two)):
-                ent_ref[2 * kind + c, rows, :] += (value * pick).astype(BF)
-
-    @pl.when(e == pl.num_programs(0) - 1)
+        g = g_s[rows, :]
+        products = []
+        for j in range(per):
+            u = jnp.dot(a2, wg_ref[j], preferred_element_type=F32)
+            w = jnp.dot(a2, wu_ref[j], preferred_element_type=F32)
+            m = lax.dot_general(g, wd_ref[j], NT, preferred_element_type=F32)
+            products.append((u, w, m))
+        dx = None
+        back_all = None
+        parts = [None] * 6
+        for j in range(per):
+            e = step * per + j
+            u, w, m = products[j]
+            here = lane[:half] == e
+            gate = jnp.sum(jnp.where(here, gates_ref[rows, :], 0.0), axis=1, keepdims=True)
+            picked = (ids_ref[rows, 0:1] == e) | (ids_ref[rows, 1:2] == e)
+            sig = 1.0 / (1.0 + jnp.exp(-u))
+            act = u * sig
+            mid = (act * w).astype(BF).astype(F32)
+            back = jnp.sum(mid * m, axis=1, keepdims=True)
+            back = jnp.where(here & picked, back, 0.0)
+            back_all = back if back_all is None else back_all + back
+            gm = gate * m
+            up_back = (gm * act).astype(BF)
+            pre_back = (gm * w * sig * (1.0 + u * (1.0 - sig))).astype(BF)
+            term = lax.dot_general(
+                pre_back, wg_ref[j], NT, preferred_element_type=F32
+            ) + lax.dot_general(up_back, wu_ref[j], NT, preferred_element_type=F32)
+            dx = term if dx is None else dx + term
+            chosen = masks(ids_ref, rows, e, half, u.shape[1])
+            for kind, value in enumerate(((mid * gate).astype(BF), pre_back, up_back)):
+                for c in range(2):
+                    part = value * chosen[c]
+                    unit = 2 * kind + c
+                    parts[unit] = part if parts[unit] is None else parts[unit] + part
+        dx_s[rows, :] += dx
+        back_s[rows, :] += back_all
+        for unit in range(6):
+            ent_ref[unit, rows, :] += parts[unit]
+
+    @pl.when(step == pl.num_programs(0) - 1)
     def _():
-        mix_keep_ref[...] = mix_s[:half, :]
-        mix_send_ref[...] = mix_s[half:, :].astype(BF)
         dx_keep_ref[:, :width] = dx_s[:half, :]
         dx_send_ref[:, :width] = dx_s[half:, :].astype(BF)
         pad = jnp.zeros((half, 128 - experts), F32)
@@ -670,28 +684,28 @@
         dx_send_ref[:, width:] = jnp.concatenate([back_s[half:, :], pad], axis=1).astype(BF)
 
 
+def whole(*shape):
+    return pl.BlockSpec(shape, lambda e: (0,) * len(shape))
+
+
+def some_of(*shape):
+    return pl.BlockSpec(shape, lambda e: (e,) + (0,) * (len(shape) - 1))
+
+
 def experts_call(core, ids, mine, theirs, g, wr, wg, wu, wd, first=()):
     half, width = mine.shape
     tok = 2 * half
     experts, _, hidden = wg.shape
-
-    def whole(*shape):
-        return pl.BlockSpec(shape, lambda e, *_: (0,) * len(shape))
-
-    def one(*shape):
-        return pl.BlockSpec((1,) + shape, lambda e, *_: (e,) + (0,) * len(shape))
-
+    per = 2
     return pl.pallas_call(
-        drop_first(experts_kernel, 9, len(first)),
+        drop_first(functools.partial(experts_kernel, per), 9, len(first)),
         out_shape=(
-            jax.ShapeDtypeStruct((half, width), F32),
-            jax.ShapeDtypeStruct((half, width), BF),
             jax.ShapeDtypeStruct((half, width + 128), F32),
             jax.ShapeDtypeStruct((half, width + 128), BF),
             jax.ShapeDtypeStruct((tok, experts), F32),
             jax.ShapeDtypeStruct((6, tok, hidden), BF),
         ),
-        grid=(experts,),
+        grid=(experts // per,),
         in_specs=[
             pl.BlockSpec(memory_space=pltpu.SMEM),
             whole(tok, 2),
@@ -699,14 +713,12 @@
             whole(half, width),
             whole(tok, width),
             whole(experts, width),
-            one(width, hidden),
-            one(width, hidden),
-            one(hidden, width),
+            some_of(per, width, hidden),
+            some_of(per, width, hidden),
+            some_of(per, hidden, width),
         ]
         + anywhere(len(first)),
         out_specs=(
-            whole(half, width),
-            whole(half, width),
             whole(half, width + 128),
             whole(half, width + 128),
             whole(tok, experts),
@@ -716,13 +728,62 @@
             pltpu.VMEM((tok, width), BF),
             pltpu.VMEM((tok, width), BF),
             pltpu.VMEM((tok, width), F32),
-            pltpu.VMEM((tok, width), F32),
             pltpu.VMEM((tok, experts), F32),
         ],
         compiler_params=params(dimension_semantics=("arbitrary",)),
         name="experts",
-        cost_estimate=cost(32),
+        cost_estimate=cost(26),
     )(core, ids, mine, theirs, g, wr, wg, wu, wd, *first)
+
+
+def mix_kernel(per, ids_ref, ent_ref, wd_ref, keep_ref, send_ref, mix_s):
+    step = pl.program_id(0)
+    half, width = keep_ref.shape
+
+    @pl.when(step == 0)
+    def _():
+        mix_s[...] = jnp.zeros(mix_s.shape, F32)
+
+    for i in range(2):
+        rows = pl.ds(i * half, half)
+        out = None
+        for j in range(per):
+            one, two = masks(ids_ref, rows, step * per + j, half, ent_ref.shape[2])
+            mid = ent_ref[0, rows, :] * one + ent_ref[1, rows, :] * two
+            term = jnp.dot(mid, wd_ref[j], preferred_element_type=F32)
+            out = term if out is None else out + term
+        mix_s[rows, :] += out
+
+    @pl.when(step == pl.num_programs(0) - 1)
+    def _():
+        keep_ref[...] = mix_s[:half, :]
+        send_ref[...] = mix_s[half:, :].astype(BF)
+
+
+def mix_call(ids, ent, wd, first=()):
+    _, tok, hidden = ent.shape
+    experts, _, width = wd.shape
+    half = tok // 2
+    per = 2
+    return pl.pallas_call(
+        drop_first(functools.partial(mix_kernel, per), 3, len(first)),
+        out_shape=(
+            jax.ShapeDtypeStruct((half, width), F32),
+            jax.ShapeDtypeStruct((half, width), BF),
+        ),
+        grid=(experts // per,),
+        in_specs=[
+            whole(tok, 2),
+            pl.BlockSpec((2, tok, hidden), lambda e: (0, 0, 0)),
+            some_of(per, hidden, width),
+        ]
+        + anywhere(len(first)),
+        out_specs=(whole(half, width), whole(half, width)),
+        scratch_shapes=[pltpu.VMEM((tok, width), F32)],
+        compiler_params=params(dimension_semantics=("arbitrary",)),
+        name="mix",
+        cost_estimate=cost(8),
+    )(ids, ent, wd, *first)
 
 
 def expert_grads_kernel(count, base, places, ids_ref, *refs):
@@ -1053,11 +1114,12 @@
     wo_chip = other_chip(output_weight)
     kv_weight = jnp.concatenate([key_weight, value_weight], axis=1)
     kv_core = other_core(kv_weight)
+    wq_core = other_core(query_weight)
     g_out = columns(owner_to, core_arr, cotangent, half, tops, side, [kv])
     if staged:
         z, y = [kv], []
         for r in range(tops - 1):
-            aside = [g_out[0], kv_core] if r == tops - 2 else []
+            aside = [g_out[0], kv_core, wq_core] if r == tops - 2 else []
             z_next, y_next = tie([hop(z[r], n_ctx, top), hop(z[r], n_ctx, low)], aside)
             z.append(z_next)
             y.append(y_next)
@@ -1095,7 +1157,7 @@
     a2_top = exchange_top(a2_out, n_ctx, digits)
     wq_chip = other_chip(query_weight)
 
-    mix_keep, mix_send, dx_keep, dx_send, gates, ent = experts_call(
+    dx_keep, dx_send, gates, ent = experts_call(
         core_arr,
         ids,
         a2_mine,
@@ -1117,7 +1179,7 @@
     if staged:
         z = [ent]
         z_next = hop(ent, n_ctx, top)
-    wq_parts = [query_weight, other_core(query_weight), wq_chip, other_core(wq_chip)]
+    wq_parts = [query_weight, wq_core, wq_chip, other_core(wq_chip)]
     hidden_grad, att_near, misc = simple(
         back_kernel,
         "back",
@@ -1132,15 +1194,15 @@
         router,
         gain_two,
         cotangent,
-        first=[wq_parts[1], wq_parts[3]],
+        first=[wq_parts[3]],
     )
     att_far = other_core(att_near)
-    (mix_send,) = tie([mix_send], [got])
+    mix_keep, mix_send = mix_call(ids, ent, down_weight, [att_near])
     mix_near = (mix_keep + other_core(mix_send).astype(F32)).astype(BF)
     mix_got = other_chip(mix_near)
     a2_pieces = exchange_rest(a2_top, n_ctx, digits)
     if staged:
-        (z_next,) = tie([z_next], [att_near])
+        (z_next,) = tie([z_next], [mix_send])
         z.append(z_next)
         z_next = hop(z[1], n_ctx, top)
 
@@ -1270,7 +1332,8 @@
     )
     in_far = other_core(in_mine)
     done = finish(0, experts, grads_a, got_a, first=[norm_row])
-    late, mix_got = tie([late, mix_got], [send_b])
+    (late,) = tie([late], [send_b])
+    (mix_got,) = tie([mix_got], [norm_row])
     out_mine = hidden_one + mix_near.astype(F32) + mix_got.astype(F32)
     out_far = other_core(out_mine)
     (layer_output,) = simple(
@@ -1282,7 +1345,7 @@
     if staged:
         blocks = cut(terms, tops)
         moving = blocks[1]
-        waits = [[send_b], [done[0]], [layer_output]]
+        waits = [[in_mine], [input_grad], [layer_output]]
         for r in range(2, tops + 1):
             (moving,) = tie([hop(moving, n_ctx, top)], waits[r - 2])
             moving = total([moving, blocks[r % tops]]).astype(BF if r < tops else F32)
@@ -1290,7 +1353,7 @@
     else:
         terms_own = scatter_ctx(terms, n_ctx, digits[1:])
     late_own = scatter_ctx(
-        late, n_ctx, digits, lambda at, xs: tie(xs, [done[0]] if at else [layer_output, input_grad])
+        late, n_ctx, digits, lambda at, xs: tie(xs, [done[0]] if at else [input_grad])
     )
     norm_rel = norm_row[0].reshape(n_ctx, cols)[owner_from]
     norm_own = scatter_ctx(norm_rel, n_ctx, digits, kind=F32)

time: 378 us -> 366 us (0.968)
  waiting for transfers between devices: 83.3 us -> 74.8 us
    ppermute x35, waiting for transfers between devices: 51.7 us -> 42.1 us  [hop(): return lax.ppermute(x, 'ctx', moved(n, digit, shift))]
    pallas_call x1 -> x2, Pallas kernels: 32.1 us -> 33.2 us  [the longest x1 25.1 us: experts_call(): pl.pallas_call(drop_first(functools.partial(experts_kernel, per), 9, len(...]
    unnamed x96 -> x104, local copies, waits for them, and re-layouts: 15 us -> 14.1 us
  transfers between devices with their start and end apart: 63 -> 63, of which waited for: 18 -> 18; matrix products, arithmetic and copies ran while one was open for 9% -> 11% of each run, Pallas kernels for 46% -> 49%
where the time goes in v1:
time: 366 us; the launch traced here: 362 us
  Pallas kernels  184 us (50%)
  waiting for transfers between devices  74.8 us (20%)
  starting transfers between devices  46.6 us (13%)
  local copies, waits for them, and re-layouts  28.4 us (8%)
  other arithmetic  26.3 us (7%)
    ppermute x35, waiting for transfers between devices, hop(): return lax.ppermute(x, 'ctx', moved(n, digit, shift))  42.1 us
    pallas_call x2, Pallas kernels, attend_back(): pl.pallas_call(drop_first(kernel, len(operands), len(first)), out_shape=t...  37.3 us
    ppermute x35, starting transfers between devices, hop(): return lax.ppermute(x, 'ctx', moved(n, digit, shift))  32.1 us
    pallas_call x6, Pallas kernels, simple(): pl.pallas_call(drop_first(kernel, 1 + len(operands), len(first)), out_sha...  31.1 us
    ppermute x8, waiting for transfers between devices, other_chip(): return lax.ppermute(x, 'wa', [(i, i ^ 2) for i in range(4)])  25.6 us
    pallas_call x1, Pallas kernels, experts_call(): pl.pallas_call(drop_first(functools.partial(experts_kernel, per), 9, len(...  25.1 us
    pallas_call x2, Pallas kernels, expert_grads(): pl.pallas_call(drop_first(kernel, len(operands), len(first)), out_shape=(...  23.8 us
    pallas_call x1, Pallas kernels, attend(): pl.pallas_call(drop_first(functools.partial(attend_kernel, nb, heads, gro...  22.2 us
  transfers between devices with their start and end apart: 63, of which 18 were waited for; matrix products, arithmetic and copies ran while one was open for 11% of the time, Pallas kernels for 49%

profile of v1, /device:TPU:0, one launch (start us, length us, event | category | flops | bytes accessed | tf_op | source)
XLA Modules:
  0.0 361.7 jit_solution(9673790738047107217)
XLA Ops:
  5.3 5.0 %project.1 = (bf16[512,1536]{1,0:T(8,128)(2,1)}, bf16[512,384]{1,0:T(8,128)(2,1)}, bf16[528,256]{1,0:T(8,128)(2,1)}) custom-call(s32[1]{0:T(128)} %bitcast.core_ref.refs_0_, bf16[512,1536]{1,0:T(8,128)(2,1)} %x_ref.7, f32[1536]{0:T(1024)} %gain_ref.5, bf16[1536,384]{1,0:T(8,128)(2,1)} %refs_2_.3, bf16[1536,128]{1,0:T(8,128)(2,1)} %wk_ref.1, ...), custom_call_target="tpu_custom_call" | custom-call | flops 1500000000 | bytes 4500000 | tf_op jit(solution)/shard_map/project/pallas_call | solution.py:241
  14.6 5.5 %collective-permute-done.1.refs_1_ = bf16[528,256]{1,0:T(8,128)(2,1)S(1)} collective-permute-done((bf16[528,256]{1,0:T(8,128)(2,1)}, bf16[528,256]{1,0:T(8,128)(2,1)S(1)}, u32[]{:S(2)}, u32[]{:S(2)}) %collective-permute-start.1) | collective-permute-done | bytes 270368 | tf_op jit(solution)/shard_map/ppermute | solution.py:49
  24.9 7.4 %collective-permute-done.3.refs_1_ = bf16[528,256]{1,0:T(8,128)(2,1)S(1)} collective-permute-done((bf16[528,256]{1,0:T(8,128)(2,1)}, bf16[528,256]{1,0:T(8,128)(2,1)S(1)}, u32[]{:S(2)}, u32[]{:S(2)}) %collective-permute-start.3) | collective-permute-done | bytes 270368 | tf_op jit(solution)/shard_map/ppermute | solution.py:49
  47.3 5.6 %collective-permute-done.8.refs_8_.refs_6_ = bf16[528,256]{1,0:T(8,128)(2,1)S(1)} collective-permute-done((bf16[528,256]{1,0:T(8,128)(2,1)}, bf16[528,256]{1,0:T(8,128)(2,1)S(1)}, u32[]{:S(2)}, u32[]{:S(2)}) %collective-permute-start.8) | collective-permute-done | bytes 270368 | tf_op jit(solution)/shard_map/ppermute | solution.py:49
  53.6 22.2 %attend.1 = (f32[512,384]{1,0:T(8,128)}, bf16[256,384]{1,0:T(8,128)(2,1)}, bf16[256,384]{1,0:T(8,128)(2,1)}, f32[8,512]{1,0:T(8,128)}) custom-call(bf16[512,384]{1,0:T(8,128)(2,1)} %get-tuple-element.104.refs_0_, bf16[528,256]{1,0:T(8,128)(2,1)} %get-tuple-element.105.refs_0_.refs_1_.refs_3_, bf16[528,256]{1,0:T(8,128)(2,1)} %get-tuple-element.106.refs_2_.refs_3_, ...), custom_call_target="tpu_custom_call" | custom-call | flops 8099999744 | bytes 24300000 | tf_op jit(solution)/shard_map/attend/pallas_call | solution.py:401
  79.2 5.8 %collective-permute-done.14.refs_2_ = bf16[256,384]{1,0:T(8,128)(2,1)S(1)} collective-permute-done((bf16[256,384]{1,0:T(8,128)(2,1)}, bf16[256,384]{1,0:T(8,128)(2,1)S(1)}, u32[]{:S(2)}, u32[]{:S(2)}) %collective-permute-start.14) | collective-permute-done | bytes 196640 | tf_op jit(solution)/shard_map/ppermute | solution.py:57
  89.1 6.3 %middle.1 = (f32[256,1536]{1,0:T(8,128)}, bf16[256,1536]{1,0:T(8,128)(2,1)}) custom-call(s32[1]{0:T(128)} %bitcast.core_ref.refs_0_, bf16[512,1536]{1,0:T(8,128)(2,1)} %x_ref.7, f32[1536]{0:T(1024)} %refs_8_.3, bf16[256,384]{1,0:T(8,128)(2,1)} %get-tuple-element.118.refs_0_.refs_3_, bf16[256,384]{1,0:T(8,128)(2,1)} %copy-done.44, ...), custom_call_target="tpu_custom_call" | custom-call | flops 1500000000 | bytes 4500000 | tf_op jit(solution)/shard_map/middle/pallas_call | solution.py:872
  103.8 25.1 %experts.1 = (f32[256,1664]{1,0:T(8,128)}, bf16[256,1664]{1,0:T(8,128)(2,1)}, f32[512,8]{1,0:T(8,128)}, bf16[6,512,256]{2,1,0:T(8,128)(2,1)}) custom-call(s32[1]{0:T(128)} %bitcast.core_ref.refs_0_, s32[512,2]{1,0:T(8,128)} %get-tuple-element.223.refs_1_.refs_6_.refs_0_, bf16[256,1536]{1,0:T(8,128)(2,1)} %get-tuple-element.122.x_ref.refs_2_.refs_4_, ...), custom_call_target="tpu_custom_call" | custom-call | flops 7800000000 | bytes 23400000 | tf_op jit(solution)/shard_map/experts/pallas_call | solution.py:700
  136.9 19.9 %collective-permute-done.24.refs_2_ = bf16[256,1664]{1,0:T(8,128)(2,1)S(1)} collective-permute-done((bf16[256,1664]{1,0:T(8,128)(2,1)S(1)}, bf16[256,1664]{1,0:T(8,128)(2,1)S(1)}, u32[]{:S(2)}, u32[]{:S(2)}) %collective-permute-start.24) | collective-permute-done | bytes 852000 | tf_op jit(solution)/shard_map/ppermute | solution.py:57
  157.6 5.6 %back.1 = (f32[256,1536]{1,0:T(8,128)}, bf16[256,1536]{1,0:T(8,128)(2,1)}, f32[16,1536]{1,0:T(8,128)}) custom-call(s32[1]{0:T(128)} %bitcast.core_ref.refs_0_, bf16[256,1664]{1,0:T(8,128)(2,1)} %copy-done.13, bf16[256,1664]{1,0:T(8,128)(2,1)} %copy-done.31, f32[256,1536]{1,0:T(8,128)} %get-tuple-element.121.refs_3_, ...), custom_call_target="tpu_custom_call" | custom-call | flops 1500000000 | bytes 4500000 | tf_op jit(solution)/shard_map/back/pallas_call | solution.py:872
  163.2 8.1 %mix.1 = (f32[256,1536]{1,0:T(8,128)}, bf16[256,1536]{1,0:T(8,128)(2,1)}) custom-call(s32[512,2]{1,0:T(8,128)} %get-tuple-element.223.refs_1_.refs_6_.refs_0_, bf16[6,512,256]{2,1,0:T(8,128)(2,1)} %get-tuple-element.124.refs_1_.refs_4_.refs_5_, bf16[8,256,1536]{2,1,0:T(8,128)(2,1)} %refs_2_.2, bf16[256,1536]{1,0:T(8,128)(2,1)} %get-tuple-element.136.refs_3_.refs_7_.refs_1_), custom_call_target="tpu_custom_call" | custom-call | flops 2400000000 | bytes 7200000 | tf_op jit(solution)/shard_map/mix/pallas_call | solution.py:768
  179.7 19.4 %attend_back.2 = (bf16[4,512,256]{2,1,0:T(8,128)(2,1)}, bf16[512,384]{1,0:T(8,128)(2,1)}, f32[8,512]{1,0:T(8,128)}, f32[4,64,768]{2,1,0:T(8,128)}) custom-call(bf16[512,384]{1,0:T(8,128)(2,1)} %get-tuple-element.104.refs_0_, bf16[528,256]{1,0:T(8,128)(2,1)} %get-tuple-element.105.refs_0_.refs_1_.refs_3_, f32[8,512]{1,0:T(8,128)} %get-tuple-element.139.refs_2_, ...), custom_call_target="tpu_custom_call" | custom-call | flops 5400000000 | bytes 16200000 | tf_op jit(solution)/shard_map/attend_back/pallas_call | solution.py:530
  206.1 4.1 %weight_terms.3.refs_1_.refs_13_ = bf16[8,192,512]{2,1,0:T(8,128)(2,1)} custom-call(s32[8]{0:T(128)} %stack.106.refs_0_, bf16[256,1536]{1,0:T(8,128)(2,1)} %get-tuple-element.136.refs_3_.refs_7_.refs_1_, bf16[256,1536]{1,0:T(8,128)(2,1)} %collective-permute-done.28.refs_8_.refs_2_, bf16[256,384]{1,0:T(8,128)(2,1)} %get-tuple-element.118.refs_0_.refs_3_, ...), custom_call_target="tpu_custom_call" | custom-call | flops 1200000000 | bytes 3600000 | tf_op jit(solution)/shard_map/weight_terms/pallas_call | solution.py:1039
  217.7 17.9 %attend_back.3 = (bf16[4,512,256]{2,1,0:T(8,128)(2,1)}, bf16[256,384]{1,0:T(8,128)(2,1)}, bf16[256,384]{1,0:T(8,128)(2,1)}) custom-call(bf16[512,384]{1,0:T(8,128)(2,1)} %get-tuple-element.104.refs_0_, bf16[528,256]{1,0:T(8,128)(2,1)} %get-tuple-element.105.refs_0_.refs_1_.refs_3_, f32[8,512]{1,0:T(8,128)} %get-tuple-element.139.refs_2_, ...), custom_call_target="tpu_custom_call" | custom-call | flops 5400000000 | bytes 16200000 | tf_op jit(solution)/shard_map/attend_back/pallas_call | solution.py:530
  240.5 3.9 %weight_terms.4.refs_2_ = bf16[8,192,384]{2,1,0:T(8,128)(2,1)} custom-call(s32[8]{0:T(128)} %stack.106.refs_0_, bf16[512,1536]{1,0:T(8,128)(2,1)} %get-tuple-element.160.refs_1_.refs_0_, bf16[512,384]{1,0:T(8,128)(2,1)} %pad_maximum_fusion.1.refs_2_, bf16[1,512,256]{2,1,0:T(8,128)(2,1)} %get-tuple-element.226.refs_3_), custom_call_target="tpu_custom_call" | custom-call | flops 1200000000 | bytes 3600000 | tf_op jit(solution)/shard_map/weight_terms/pallas_call | solution.py:1039
  256.3 12.0 %expert_grads.2 = (f32[4,192,256]{2,1,0:T(8,128)}, f32[4,192,256]{2,1,0:T(8,128)}, f32[4,192,256]{2,1,0:T(8,128)}, bf16[3,4,192,256]{3,2,1,0:T(8,128)(2,1)}) custom-call(f32[4,512,8]{2,1,0:T(8,128)} %routes.1.refs_10_.ids_ref.refs_0_, bf16[4,384,256]{2,1,0:T(8,128)(2,1)} %stacked.2.refs_7_.refs_0_.refs_1_, ...), custom_call_target="tpu_custom_call" | custom-call | flops 1440000000 | bytes 4320000 | tf_op jit(solution)/shard_map/expert_grads/pallas_call | solution.py:824
  275.1 5.6 %query_back.1.refs_3_.query_ref = f32[256,1536]{1,0:T(8,128)} custom-call(s32[1]{0:T(128)} %bitcast.core_ref.refs_0_, bf16[2,256,384]{2,1,0:T(8,128)(2,1)} %get-tuple-element.167.refs_0_, bf16[2,256,384]{2,1,0:T(8,128)(2,1)} %tie.39.refs_1_, bf16[1536,384]{1,0:T(8,128)(2,1)} %refs_2_.3, bf16[1536,384]{1,0:T(8,128)(2,1)} %copy-done.11, ...), custom_call_target="tpu_custom_call" | custom-call | flops 1500000000 | bytes 4500000 | tf_op jit(solution)/shard_map/query_back/pallas_call | solution.py:872
  287.7 11.9 %expert_grads.3 = (f32[4,192,256]{2,1,0:T(8,128)}, f32[4,192,256]{2,1,0:T(8,128)}, f32[4,192,256]{2,1,0:T(8,128)}, bf16[3,4,192,256]{3,2,1,0:T(8,128)(2,1)}) custom-call(f32[4,512,8]{2,1,0:T(8,128)} %routes.1.refs_10_.ids_ref.refs_0_, bf16[4,384,256]{2,1,0:T(8,128)(2,1)} %stacked.2.refs_7_.refs_0_.refs_1_, ...), custom_call_target="tpu_custom_call" | custom-call | flops 1440000000 | bytes 4320000 | tf_op jit(solution)/shard_map/expert_grads/pallas_call | solution.py:824
  306.2 6.1 %input.1 = (f32[256,1536]{1,0:T(8,128)}, f32[8,1536]{1,0:T(8,128)}) custom-call(s32[1]{0:T(128)} %bitcast.core_ref.refs_0_, bf16[512,1536]{1,0:T(8,128)(2,1)} %x_ref.7, f32[1536]{0:T(1024)} %gain_ref.5, f32[256,1536]{1,0:T(8,128)} %get-tuple-element.143.grad_ref, f32[256,1536]{1,0:T(8,128)} %query_back.1.refs_3_.query_ref, bf16[256,256]{1,0:T(8,128)(2,1)} %copy-done.34, ...), custom_call_target="tpu_custom_call" | custom-call | flops 1500000000 | bytes 4500000 | tf_op jit(solution)/shard_map/input/pallas_call | solution.py:872
  327.3 4.2 %finish.2 = (f32[8,192,256]{2,1,0:T(8,128)}, f32[8,192,256]{2,1,0:T(8,128)}, f32[8,192,256]{2,1,0:T(8,128)}) custom-call(f32[4,192,256]{2,1,0:T(8,128)} %get-tuple-element.180.refs_0_, f32[4,192,256]{2,1,0:T(8,128)} %get-tuple-element.181.refs_1_, f32[4,192,256]{2,1,0:T(8,128)} %get-tuple-element.182.refs_2_, ...), custom_call_target="tpu_custom_call" | custom-call | flops 900000000 | bytes 2700000 | tf_op jit(solution)/shard_map/finish/pallas_call | solution.py:851
  335.8 4.2 %finish.3 = (f32[8,192,256]{2,1,0:T(8,128)}, f32[8,192,256]{2,1,0:T(8,128)}, f32[8,192,256]{2,1,0:T(8,128)}) custom-call(f32[4,192,256]{2,1,0:T(8,128)} %get-tuple-element.188.refs_0_, f32[4,192,256]{2,1,0:T(8,128)} %get-tuple-element.189.refs_1_, ...), custom_call_target="tpu_custom_call", output_to_operand_aliasing={{0}: (4, {}), {1}: (5, {}), {2}: (6, {})} | custom-call | flops 900000000 | bytes 2700000 | tf_op jit(solution)/shard_map/finish/pallas_call | solution.py:851
  339.9 3.8 %place.3.refs_1_ = f32[512,1536]{1,0:T(8,128)} custom-call(s32[1]{0:T(128)} %bitcast.core_ref.refs_0_, f32[256,1536]{1,0:T(8,128)} %get-tuple-element.179.mine_ref.refs_1_, f32[256,1536]{1,0:T(8,128)} %collective-permute-done.49.theirs_ref), custom_call_target="tpu_custom_call" | custom-call | flops 1500000000 | bytes 4500000 | tf_op jit(solution)/shard_map/place/pallas_call | solution.py:872
  348.1 3.8 %place.2.refs_1_ = f32[512,1536]{1,0:T(8,128)} custom-call(s32[1]{0:T(128)} %bitcast.core_ref.refs_0_, f32[256,1536]{1,0:T(8,128)} %copy-done.8, f32[256,1536]{1,0:T(8,128)} %collective-permute-done.48.theirs_ref), custom_call_target="tpu_custom_call" | custom-call | flops 1500000000 | bytes 4500000 | tf_op jit(solution)/shard_map/place/pallas_call | solution.py:872
  352.6 4.4 %collective-permute-done.52.refs_0_ = bf16[1,192,896]{2,1,0:T(8,128)(2,1)S(1)} collective-permute-done((bf16[1,192,896]{2,1,0:T(8,128)(2,1)}, bf16[1,192,896]{2,1,0:T(8,128)(2,1)S(1)}, u32[]{:S(2)}, u32[]{:S(2)}) %collective-permute-start.52) | collective-permute-done | bytes 344096 | tf_op jit(solution)/shard_map/ppermute | solution.py:49
  (307 shorter events, 142.5 us)
Async XLA Ops:
  0.7 44.4 %collective-permute-start.7 = (bf16[1536,384]{1,0:T(8,128)(2,1)}, bf16[1536,384]{1,0:T(8,128)(2,1)S(1)}, u32[]{:S(2)}, u32[]{:S(2)}) collective-permute-start(bf16[1536,384]{1,0:T(8,128)(2,1)} %refs_2_.3), channel_id=1, source_target_pairs={{0,1},{1,0},{2,3},{3,2},{4,5},{5,4},{6,7},{7,6},{8,9},{9,8},{10,11... | collective-permute-start | bytes 3538952 | tf_op jit(solution)/shard_map/ppermute | solution.py:53
  14.6 26.7 %collective-permute-start.6 = (bf16[1536,256]{1,0:T(8,128)(2,1)S(1)}, bf16[1536,256]{1,0:T(8,128)(2,1)}, u32[]{:S(2)}, u32[]{:S(2)}) collective-permute-start(bf16[1536,256]{1,0:T(8,128)(2,1)S(1)} %constant_dynamic-update-slice_fusion.refs_0_), channel_id=1, source_target_pairs={{0,1},{1,0},{2,3},{3,2},{4,5},{5,4},{6,7},{7,6},{8,9},{9,8},{10,11... | collective-permute-start | bytes 2359304 | tf_op jit(solution)/shard_map/ppermute | solution.py:53
  36.5 39.4 %collective-permute-start.9 = (bf16[384,1536]{1,0:T(8,128)(2,1)}, bf16[384,1536]{1,0:T(8,128)(2,1)S(1)}, u32[]{:S(2)}, u32[]{:S(2)}) collective-permute-start(bf16[384,1536]{1,0:T(8,128)(2,1)} %refs_9_.3), channel_id=1, source_target_pairs={{0,2},{1,3},{2,0},{3,1},{4,6},{5,7},{6,4},{7,5},{8,10},{9,11},{10,... | collective-permute-start | bytes 3538952 | tf_op jit(solution)/shard_map/ppermute | solution.py:57
  47.1 32.1 %collective-permute-start.16 = (bf16[384,1536]{1,0:T(8,128)(2,1)}, bf16[384,1536]{1,0:T(8,128)(2,1)S(1)}, u32[]{:S(2)}, u32[]{:S(2)}) collective-permute-start(bf16[384,1536]{1,0:T(8,128)(2,1)} %refs_9_.3), channel_id=1, source_target_pairs={{0,1},{1,0},{2,3},{3,2},{4,5},{5,4},{6,7},{7,6},{8,9},{9,8},{10,11... | collective-permute-start | bytes 3538952 | tf_op jit(solution)/shard_map/ppermute | solution.py:53
  47.1 28.7 %collective-permute-start.10 = (bf16[1,384,256]{2,1,0:T(8,128)(2,1)S(1)}, bf16[1,384,256]{2,1,0:T(8,128)(2,1)S(1)}, u32[]{:S(2)}, u32[]{:S(2)}) collective-permute-start(bf16[1,384,256]{2,1,0:T(8,128)(2,1)S(1)} %copy-done.50), channel_id=1, source_target_pairs={{0,8},{4,12},{8,16},{12,20},{16,24},{20,28},{24,0},{28,4},{1,9},{5... | collective-permute-start | bytes 589832 | tf_op jit(solution)/shard_map/ppermute | solution.py:49
  47.1 28.7 %collective-permute-start.11 = (bf16[1,384,256]{2,1,0:T(8,128)(2,1)S(1)}, bf16[1,384,256]{2,1,0:T(8,128)(2,1)S(1)}, u32[]{:S(2)}, u32[]{:S(2)}) collective-permute-start(bf16[1,384,256]{2,1,0:T(8,128)(2,1)S(1)} %copy-done.49), channel_id=1, source_target_pairs={{0,16},{4,20},{8,24},{12,28},{16,0},{20,4},{24,8},{28,12},{1,17},{... | collective-permute-start | bytes 589832 | tf_op jit(solution)/shard_map/ppermute | solution.py:49
  95.7 33.2 %collective-permute-start.19 = (bf16[1536,384]{1,0:T(8,128)(2,1)S(1)}, bf16[1536,384]{1,0:T(8,128)(2,1)S(1)}, u32[]{:S(2)}, u32[]{:S(2)}) collective-permute-start(bf16[1536,384]{1,0:T(8,128)(2,1)S(1)} %copy-done.27), channel_id=1, source_target_pairs={{0,2},{1,3},{2,0},{3,1},{4,6},{5,7},{6,4},{7,5},{8,10},{9,11},{10,... | collective-permute-start | bytes 3538952 | tf_op jit(solution)/shard_map/ppermute | solution.py:57
  99.5 29.4 %collective-permute-start.20 = (bf16[1,384,256]{2,1,0:T(8,128)(2,1)}, bf16[1,384,256]{2,1,0:T(8,128)(2,1)S(1)}, u32[]{:S(2)}, u32[]{:S(2)}) collective-permute-start(bf16[1,384,256]{2,1,0:T(8,128)(2,1)} %get-tuple-element.127), channel_id=1, source_target_pairs={{0,8},{4,12},{8,16},{12,20},{16,24},{20,28},{24,0},{28,4},{1,9},{5... | collective-permute-start | bytes 589832 | tf_op jit(solution)/shard_map/ppermute | solution.py:49
  100.1 28.8 %collective-permute-start.21 = (bf16[1,384,256]{2,1,0:T(8,128)(2,1)}, bf16[1,384,256]{2,1,0:T(8,128)(2,1)S(1)}, u32[]{:S(2)}, u32[]{:S(2)}) collective-permute-start(bf16[1,384,256]{2,1,0:T(8,128)(2,1)} %get-tuple-element.128), channel_id=1, source_target_pairs={{0,16},{4,20},{8,24},{12,28},{16,0},{20,4},{24,8},{28,12},{1,17},{... | collective-permute-start | bytes 589832 | tf_op jit(solution)/shard_map/ppermute | solution.py:49
  100.1 28.8 %collective-permute-start.22 = (bf16[1,384,256]{2,1,0:T(8,128)(2,1)}, bf16[1,384,256]{2,1,0:T(8,128)(2,1)S(1)}, u32[]{:S(2)}, u32[]{:S(2)}) collective-permute-start(bf16[1,384,256]{2,1,0:T(8,128)(2,1)} %get-tuple-element.129), channel_id=1, source_target_pairs={{0,24},{4,28},{8,0},{12,4},{16,8},{20,12},{24,16},{28,20},{1,25},{... | collective-permute-start | bytes 589832 | tf_op jit(solution)/shard_map/ppermute | solution.py:49
  136.3 38.0 %collective-permute-start.29 = (bf16[6,512,256]{2,1,0:T(8,128)(2,1)S(1)}, bf16[6,512,256]{2,1,0:T(8,128)(2,1)S(1)}, u32[]{:S(2)}, u32[]{:S(2)}) collective-permute-start(bf16[6,512,256]{2,1,0:T(8,128)(2,1)S(1)} %copy-done.3), channel_id=1, source_target_pairs={{0,8},{4,12},{8,16},{12,20},{16,24},{20,28},{24,0},{28,4},{1,9},{5... | collective-permute-start | bytes 4718600 | tf_op jit(solution)/shard_map/ppermute | solution.py:49
  175.4 37.4 %collective-permute-start.30 = (bf16[6,512,256]{2,1,0:T(8,128)(2,1)}, bf16[6,512,256]{2,1,0:T(8,128)(2,1)S(1)}, u32[]{:S(2)}, u32[]{:S(2)}) collective-permute-start(bf16[6,512,256]{2,1,0:T(8,128)(2,1)} %tie.30.refs_12_.refs_5_.refs_6_), channel_id=1, source_target_pairs={{0,8},{4,12},{8,16},{12,20},{16,24},{20,28},{24,0},{28,4},{1,9},{5... | collective-permute-start | bytes 4718600 | tf_op jit(solution)/shard_map/ppermute | solution.py:49
  204.0 31.6 %collective-permute-start.36 = (bf16[4,512,256]{2,1,0:T(8,128)(2,1)}, bf16[4,512,256]{2,1,0:T(8,128)(2,1)}, u32[]{:S(2)}, u32[]{:S(2)}) collective-permute-start(bf16[4,512,256]{2,1,0:T(8,128)(2,1)} %get-tuple-element.161), channel_id=1, source_target_pairs={{0,4},{4,0},{8,12},{12,8},{16,20},{20,16},{24,28},{28,24},{1,5},{5... | collective-permute-start | bytes 3145736 | tf_op jit(solution)/shard_map/ppermute | solution.py:49
  204.9 30.7 %collective-permute-start.37 = (bf16[1536,256]{1,0:T(8,128)(2,1)}, bf16[1536,256]{1,0:T(8,128)(2,1)}, u32[]{:S(2)}, u32[]{:S(2)}) collective-permute-start(bf16[1536,256]{1,0:T(8,128)(2,1)} %get-tuple-element.162.refs_4_), channel_id=1, source_target_pairs={{0,2},{1,3},{2,0},{3,1},{4,6},{5,7},{6,4},{7,5},{8,10},{9,11},{10,... | collective-permute-start | bytes 2359304 | tf_op jit(solution)/shard_map/ppermute | solution.py:57
  214.0 39.7 %collective-permute-start.31 = (bf16[6,512,256]{2,1,0:T(8,128)(2,1)}, bf16[6,512,256]{2,1,0:T(8,128)(2,1)S(1)}, u32[]{:S(2)}, u32[]{:S(2)}) collective-permute-start(bf16[6,512,256]{2,1,0:T(8,128)(2,1)} %tie.35.refs_14_.refs_6_.refs_7_), channel_id=1, source_target_pairs={{0,8},{4,12},{8,16},{12,20},{16,24},{20,28},{24,0},{28,4},{1,9},{5... | collective-permute-start | bytes 4718600 | tf_op jit(solution)/shard_map/ppermute | solution.py:49
  217.6 30.9 %collective-permute-start.35 = (bf16[4,192,512]{2,1,0:T(8,128)(2,1)}, bf16[4,192,512]{2,1,0:T(8,128)(2,1)S(1)}, u32[]{:S(2)}, u32[]{:S(2)}) collective-permute-start(bf16[4,192,512]{2,1,0:T(8,128)(2,1)} %slice.194), channel_id=1, source_target_pairs={{0,4},{4,0},{8,12},{12,8},{16,20},{20,16},{24,28},{28,24},{1,5},{5... | collective-permute-start | bytes 2359304 | tf_op jit(solution)/shard_map/ppermute | solution.py:49
  248.5 32.1 %collective-permute-start.40 = (bf16[1,512,256]{2,1,0:T(8,128)(2,1)}, bf16[1,512,256]{2,1,0:T(8,128)(2,1)}, u32[]{:S(2)}, u32[]{:S(2)}) collective-permute-start(bf16[1,512,256]{2,1,0:T(8,128)(2,1)} %get-tuple-element.226.refs_3_), channel_id=1, source_target_pairs={{0,24},{4,28},{8,0},{12,4},{16,8},{20,12},{24,16},{28,20},{1,25},{... | collective-permute-start | bytes 786440 | tf_op jit(solution)/shard_map/ppermute | solution.py:49
  248.8 31.9 %collective-permute-start.42 = (bf16[1,512,256]{2,1,0:T(8,128)(2,1)}, bf16[1,512,256]{2,1,0:T(8,128)(2,1)}, u32[]{:S(2)}, u32[]{:S(2)}) collective-permute-start(bf16[1,512,256]{2,1,0:T(8,128)(2,1)} %get-tuple-element.224), channel_id=1, source_target_pairs={{0,8},{4,12},{8,16},{12,20},{16,24},{20,28},{24,0},{28,4},{1,9},{5... | collective-permute-start | bytes 786440 | tf_op jit(solution)/shard_map/ppermute | solution.py:49
  250.8 29.8 %collective-permute-start.41 = (bf16[1,512,256]{2,1,0:T(8,128)(2,1)}, bf16[1,512,256]{2,1,0:T(8,128)(2,1)}, u32[]{:S(2)}, u32[]{:S(2)}) collective-permute-start(bf16[1,512,256]{2,1,0:T(8,128)(2,1)} %get-tuple-element.225), channel_id=1, source_target_pairs={{0,16},{4,20},{8,24},{12,28},{16,0},{20,4},{24,8},{28,12},{1,17},{... | collective-permute-start | bytes 786440 | tf_op jit(solution)/shard_map/ppermute | solution.py:49
  269.8 36.3 %collective-permute-start.46 = (bf16[3,4,192,256]{3,2,1,0:T(8,128)(2,1)S(1)}, bf16[3,4,192,256]{3,2,1,0:T(8,128)(2,1)}, u32[]{:S(2)}, u32[]{:S(2)}) collective-permute-start(bf16[3,4,192,256]{3,2,1,0:T(8,128)(2,1)S(1)} %copy-done.7), channel_id=1, source_target_pairs={{0,4},{4,0},{8,12},{12,8},{16,20},{20,16},{24,28},{28,24},{1,5},{5... | collective-permute-start | bytes 3538952 | tf_op jit(solution)/shard_map/ppermute | solution.py:49
  273.6 42.5 %collective-permute-start.50 = (bf16[1,192,896]{2,1,0:T(8,128)(2,1)}, bf16[1,192,896]{2,1,0:T(8,128)(2,1)}, u32[]{:S(2)}, u32[]{:S(2)}) collective-permute-start(bf16[1,192,896]{2,1,0:T(8,128)(2,1)} %fusion), channel_id=1, source_target_pairs={{0,8},{4,12},{8,16},{12,20},{16,24},{20,28},{24,0},{28,4},{1,9},{5... | collective-permute-start | bytes 1032200 | tf_op jit(solution)/shard_map/ppermute | solution.py:49
  301.5 34.2 %collective-permute-start.62 = (bf16[3,4,192,256]{3,2,1,0:T(8,128)(2,1)}, bf16[3,4,192,256]{3,2,1,0:T(8,128)(2,1)}, u32[]{:S(2)}, u32[]{:S(2)}) collective-permute-start(bf16[3,4,192,256]{3,2,1,0:T(8,128)(2,1)} %get-tuple-element.174.refs_4_.refs_1_), channel_id=1, source_target_pairs={{0,4},{4,0},{8,12},{12,8},{16,20},{20,16},{24,28},{28,24},{1,5},{5... | collective-permute-start | bytes 3538952 | tf_op jit(solution)/shard_map/ppermute | solution.py:49
  312.3 27.6 %collective-permute-start.49 = (f32[256,1536]{1,0:T(8,128)}, f32[256,1536]{1,0:T(8,128)}, u32[]{:S(2)}, u32[]{:S(2)}) collective-permute-start(f32[256,1536]{1,0:T(8,128)} %get-tuple-element.179.mine_ref.refs_1_), channel_id=1, source_target_pairs={{0,1},{1,0},{2,3},{3,2},{4,5},{5,4},{6,7},{7,6},{8,9},{9,8},{10,11... | collective-permute-start | bytes 4718600 | tf_op jit(solution)/shard_map/ppermute | solution.py:53
  319.8 28.3 %collective-permute-start.48 = (f32[256,1536]{1,0:T(8,128)S(1)}, f32[256,1536]{1,0:T(8,128)}, u32[]{:S(2)}, u32[]{:S(2)}) collective-permute-start(f32[256,1536]{1,0:T(8,128)S(1)} %convert_add_fusion.mine_ref), channel_id=1, source_target_pairs={{0,1},{1,0},{2,3},{3,2},{4,5},{5,4},{6,7},{7,6},{8,9},{9,8},{10,11... | collective-permute-start | bytes 4718600 | tf_op jit(solution)/shard_map/ppermute | solution.py:53
  (90 other events, 684.0 us)
